TPU v7x, 512 devices: a whole 4x8x8 slice. The times are simulated.
512 devices in a mesh: lat: 16 (over x_lo, z), lon: 32 (over x_hi, y, core).
Axes of the slice: x: 4 (x_hi: 2, x_lo: 2; x = x_hi * 2 + x_lo), y: 8, z: 8, core: 2. Of those that a mesh axis runs over, the one named last changes fastest.
Arguments:
- fields: bfloat16 [75, 128, 4096], P(None, 'lat', 'lon'), may hold values from -6 to 6
- mask: int32 [128, 4096], P('lat', 'lon'), may hold values from 0 to 1, as said below
- w1: bfloat16 [9, 48, 75], replicated, may hold values from -0.25 to 0.25
- w2: bfloat16 [9, 48, 48], replicated, may hold values from -0.3125 to 0.3125
- cotangent: bfloat16 [48, 128, 4096], P(None, 'lat', 'lon'), may hold values from -6 to 6
Outputs:
- output: bfloat16 [48, 128, 4096], P(None, 'lat', 'lon')
- dx: bfloat16 [75, 128, 4096], P(None, 'lat', 'lon')
- dw1: float32 [9, 48, 75], replicated
- dw2: float32 [9, 48, 48], replicated
Inputs may be any that keep to these rules, and one draw needn't show every extreme that they name: `mask`: rows below 8 are sea. Each aligned block of 8 x 8 grid points is all land or all sea.
All inputs are finite; a program needn't handle non-finite values.
Results may differ from a plain program's by a relative error of at most 0.017.
Values may be sent and summed in bfloat16 or wider, within the bound.
A program may use at most 64 MiB of HBM per device.

v0:
```python
import math

import jax
import jax.numpy as jnp
from jax import lax
from jax.sharding import PartitionSpec as P


def from_partner(x, axis, bit):
    return lax.ppermute(x, axis, [(i, i ^ 1 << bit) for i in range(lax.axis_size(axis))])


def extended(x, sides, width, wrap):
    for axis, dim in sides:
        peers, length = (lax.axis_size(axis), x.shape[dim])
        up = [(i, (i + 1) % peers) for i in range(peers if wrap else peers - 1)]
        down = [(j, i) for i, j in up]
        last = lax.slice_in_dim(x, length - width, length, axis=dim)
        leading = lax.slice_in_dim(x, 0, width, axis=dim)
        before = lax.ppermute(last, axis, up)
        after = lax.ppermute(leading, axis, down)
        x = jnp.concatenate([before, x, after], axis=dim)
    return x


def gelu_parts(a):
    coeff = 0.7978845608
    inner = coeff * (a + 0.044715 * a * a * a)
    tval = jnp.tanh(inner)
    value = 0.5 * a * (1.0 + tval)
    slope = 0.5 * (1.0 + tval) + 0.5 * a * (1.0 - tval * tval) * coeff * (1.0 + 0.134145 * a * a)
    return (value, slope)


def at_top():
    return lax.axis_index("lat") == lax.axis_size("lat") - 1


def bit_order():
    count = lax.axis_size("lon").bit_length() - 1
    return list(range(count))


def mirror_fwd(row_top):
    moved = row_top
    for bitnum in bit_order():
        moved = from_partner(moved, "lon", bitnum)
    return moved[:, ::-1]


def mirror_back(row_top):
    moved = row_top
    for bitnum in bit_order():
        moved = from_partner(moved.astype(jnp.bfloat16), "lon", bitnum).astype(moved.dtype)
    return moved[:, ::-1]


def extend(field):
    rows_ext = extended(field, (("lat", 1),), 1, False)
    folded = mirror_fwd(field[:, -1, :])
    top_row = jnp.where(at_top(), folded, rows_ext[:, -1, :])
    rows_ext = jnp.concatenate([rows_ext[:, :-1, :], top_row[:, None, :]], axis=1)
    return extended(rows_ext, (("lon", 2),), 1, True)


def retract(padded):
    edges = jnp.stack((padded[:, :, 0], padded[:, :, -1]), 0)
    edge_got = extended(edges, (("lon", 0),), 1, True)
    inner = padded[:, :, 1:-1]
    inner = inner.at[:, :, 0].add(edge_got[0]).at[:, :, -1].add(edge_got[3])
    rims = jnp.stack((inner[:, 0, :], inner[:, -1, :]), 0)
    rim_got = extended(rims.astype(jnp.bfloat16), (("lat", 0),), 1, False).astype(rims.dtype)
    folded = mirror_back(inner[:, -1, :])
    result = inner[:, 1:-1, :]
    top_add = rim_got[3] + jnp.where(at_top(), folded, 0.0)
    return result.at[:, 0, :].add(rim_got[0]).at[:, -1, :].add(top_add)


def conv(padded, kernel):
    rows_n = padded.shape[1] - 2
    cols_n = padded.shape[2] - 2
    total = jnp.zeros((kernel.shape[1], rows_n, cols_n), jnp.float32)
    for tap in range(9):
        drow, dcol = (tap // 3, tap % 3)
        total = total + jnp.einsum(
            "oi,ihw->ohw",
            kernel[tap],
            padded[:, drow : drow + rows_n, dcol : dcol + cols_n],
            preferred_element_type=jnp.float32,
        )
    return total


def tconv(grad, kernel):
    rows_n = grad.shape[1]
    cols_n = grad.shape[2]
    wide = jnp.pad(grad, ((0, 0), (2, 2), (2, 2)))
    total = jnp.zeros((kernel.shape[2], rows_n + 2, cols_n + 2), jnp.float32)
    for tap in range(9):
        drow, dcol = (tap // 3, tap % 3)
        total = total + jnp.einsum(
            "oi,ohw->ihw",
            kernel[tap],
            wide[:, 2 - drow : 4 - drow + rows_n, 2 - dcol : 4 - dcol + cols_n],
            preferred_element_type=jnp.float32,
        )
    return total


def wgrad(grad, padded):
    rows_n = grad.shape[1]
    cols_n = grad.shape[2]
    terms = []
    for tap in range(9):
        drow, dcol = (tap // 3, tap % 3)
        terms.append(
            jnp.einsum(
                "ohw,ihw->oi",
                grad,
                padded[:, drow : drow + rows_n, dcol : dcol + cols_n],
                preferred_element_type=jnp.float32,
            )
        )
    return jnp.stack(terms, 0)


def body(fields, mask, w1, w2, cotangent):
    sea = mask.astype(jnp.float32)
    x_ext = extend(fields)
    value, slope = gelu_parts(conv(x_ext, w1))
    hidden = (value * sea).astype(jnp.bfloat16)
    gate = slope * sea
    h_ext = extend(hidden)
    out_block = (conv(h_ext, w2) * sea).astype(jnp.bfloat16)
    grad_out = cotangent * mask.astype(jnp.bfloat16)
    term_w2 = wgrad(grad_out, h_ext)
    grad_h_ext = tconv(grad_out, w2)
    grad_h = retract(grad_h_ext)
    grad_a = (grad_h * gate).astype(jnp.bfloat16)
    term_w1 = wgrad(grad_a, x_ext)
    grad_x_ext = tconv(grad_a, w1)
    dx = retract(grad_x_ext).astype(jnp.bfloat16)
    grad_w1, grad_w2 = lax.psum((term_w1, term_w2), ("lat", "lon"))
    cells = fields.shape[1] * fields.shape[2] * lax.axis_size("lat") * lax.axis_size("lon")
    factor = 1.0 / math.sqrt(cells)
    return (out_block, dx, grad_w1 * factor, grad_w2 * factor)


def solution(mesh):
    in_specs = (P(None, "lat", "lon"), P("lat", "lon"), P(), P(), P(None, "lat", "lon"))
    out_specs = (P(None, "lat", "lon"), P(None, "lat", "lon"), P(), P())
    return jax.shard_map(body, mesh=mesh, in_specs=in_specs, out_specs=out_specs, check_vma=False)
```

profile of v0, /device:TPU:1, one launch (start us, length us, event | category | flops | bytes accessed | tf_op | source)
XLA Modules:
  0.0 454.7 jit_solution(2405748562817227738)
XLA Ops:
  11.8 4.6 %collective-permute-start.18 = (f32[1,48,10]{1,0,2:T(1,128)S(1)}, f32[1,48,10]{1,0,2:T(1,128)S(1)}, u32[]{:S(2)}, u32[]{:S(2)}) collective-permute-start(f32[1,48,10]{1,0,2:T(1,128)S(1)} %stack_squeeze.28), channel_id=1, source_target_pairs={{0,1},{1,2},{2,3},{3,4},{4,5},{5,6},{6,7},{7,8},{8,9},{9,10},{10,1... | collective-permute-start | bytes 5768 | tf_op jit(solution)/shard_map/ppermute | solution.py:20
  16.4 6.1 %collective-permute-start.19 = (f32[1,48,10]{1,0,2:T(1,128)S(1)}, f32[1,48,10]{1,0,2:T(1,128)S(1)}, u32[]{:S(2)}, u32[]{:S(2)}) collective-permute-start(f32[1,48,10]{1,0,2:T(1,128)S(1)} %stack_squeeze.29), channel_id=1, source_target_pairs={{1,0},{2,1},{3,2},{4,3},{5,4},{6,5},{7,6},{8,7},{9,8},{10,9},{11,1... | collective-permute-start | bytes 5768 | tf_op jit(solution)/shard_map/ppermute | solution.py:21
  22.7 7.3 %collective-permute-start.1 = (bf16[75,128]{0,1:T(8,128)(2,1)S(1)}, bf16[75,128]{0,1:T(8,128)(2,1)S(1)}, u32[]{:S(2)}, u32[]{:S(2)}) collective-permute-start(bf16[75,128]{0,1:T(8,128)(2,1)S(1)} %bitcast.327), channel_id=1, source_target_pairs={{0,1},{1,0},{2,3},{3,2},{4,5},{5,4},{6,7},{7,6},{8,9},{9,8},{10,11... | collective-permute-start | bytes 57608 | tf_op jit(solution)/shard_map/ppermute | solution.py:10
  31.9 1.9 collective-permute-start.2
  33.8 1.9 collective-permute-start.22
  36.9 3.4 collective-permute-start.23
  40.3 1.9 collective-permute-start.3
  43.5 4.3 collective-permute-start.24
  47.8 4.0 collective-permute-start.20
  51.8 1.9 collective-permute-start
  55.4 2.8 collective-permute-start.25
  58.1 6.4 %collective-permute-start.4 = (bf16[75,128]{0,1:T(8,128)(2,1)S(1)}, bf16[75,128]{0,1:T(8,128)(2,1)S(1)}, u32[]{:S(2)}, u32[]{:S(2)}) collective-permute-start(bf16[75,128]{0,1:T(8,128)(2,1)S(1)} %collective-permute-done.3), channel_id=1, source_target_pairs={{0,8},{1,9},{2,10},{3,11},{4,12},{5,13},{6,14},{7,15},{8,0},{9,1},... | collective-permute-start | bytes 57608 | tf_op jit(solution)/shard_map/ppermute | solution.py:10
  64.7 2.0 collective-permute-start.26
  66.9 4.8 %collective-permute-start.5 = (bf16[75,128]{0,1:T(8,128)(2,1)S(1)}, bf16[75,128]{0,1:T(8,128)(2,1)S(1)}, u32[]{:S(2)}, u32[]{:S(2)}) collective-permute-start(bf16[75,128]{0,1:T(8,128)(2,1)S(1)} %collective-permute-done.4), channel_id=1, source_target_pairs={{0,16},{1,17},{2,18},{3,19},{4,20},{5,21},{6,22},{7,23},{8,24},{9,... | collective-permute-start | bytes 57608 | tf_op jit(solution)/shard_map/ppermute | solution.py:10
  73.4 6.0 %collective-permute-start.8 = (bf16[75,10,1]{2,0,1:T(8,128)(2,1)S(1)}, bf16[75,10,1]{2,0,1:T(8,128)(2,1)S(1)}, u32[]{:S(2)}, u32[]{:S(2)}) collective-permute-start(bf16[75,10,1]{2,0,1:T(8,128)(2,1)S(1)} %get-tuple-element.134), channel_id=1, source_target_pairs={{1,0},{2,1},{3,2},{4,3},{5,4},{6,5},{7,6},{8,7},{9,8},{10,9},{11,1... | collective-permute-start | bytes 4508 | tf_op jit(solution)/shard_map/ppermute | solution.py:21
  79.5 3.1 collective-permute-start.7
  88.0 4.5 collective-permute-start.9
  92.5 7.7 %collective-permute-start.10 = (bf16[48,128]{1,0:T(8,128)(2,1)S(1)}, bf16[48,128]{1,0:T(8,128)(2,1)S(1)}, u32[]{:S(2)}, u32[]{:S(2)}) collective-permute-start(bf16[48,128]{1,0:T(8,128)(2,1)S(1)} %get-tuple-element.145), channel_id=1, source_target_pairs={{0,1},{1,0},{2,3},{3,2},{4,5},{5,4},{6,7},{7,6},{8,9},{9,8},{10,11... | collective-permute-start | bytes 36872 | tf_op jit(solution)/shard_map/ppermute | solution.py:10
  106.6 1.9 collective-permute-start.27
  108.8 2.4 collective-permute-start.28
  111.3 2.7 collective-permute-done.28
  114.1 1.9 collective-permute-start.11
  116.1 5.3 %collective-permute-start.31 = (bf16[75,128]{0,1:T(8,128)(2,1)S(1)}, bf16[75,128]{0,1:T(8,128)(2,1)S(1)}, u32[]{:S(2)}, u32[]{:S(2)}) collective-permute-start(bf16[75,128]{0,1:T(8,128)(2,1)S(1)} %get-tuple-element.126), channel_id=1, source_target_pairs={{0,1},{1,0},{2,3},{3,2},{4,5},{5,4},{6,7},{7,6},{8,9},{9,8},{10,11... | collective-permute-start | bytes 57608 | tf_op jit(solution)/shard_map/ppermute | solution.py:10
  125.5 6.1 %collective-permute-start.29 = (bf16[1,75,128]{1,2,0:T(8,128)(2,1)S(1)}, bf16[1,75,128]{1,2,0:T(8,128)(2,1)S(1)}, u32[]{:S(2)}, u32[]{:S(2)}) collective-permute-start(bf16[1,75,128]{1,2,0:T(8,128)(2,1)S(1)} %get-tuple-element.128), channel_id=1, source_target_pairs={{0,32},{32,64},{64,96},{96,128},{128,160},{160,192},{192,224},{224... | collective-permute-start | bytes 57608 | tf_op jit(solution)/shard_map/ppermute | solution.py:20
  131.6 3.6 collective-permute-start.32
  135.3 8.4 %collective-permute-start.13 = (bf16[48,128]{1,0:T(8,128)(2,1)S(1)}, bf16[48,128]{1,0:T(8,128)(2,1)S(1)}, u32[]{:S(2)}, u32[]{:S(2)}) collective-permute-start(bf16[48,128]{1,0:T(8,128)(2,1)S(1)} %collective-permute-done.12), channel_id=1, source_target_pairs={{0,8},{1,9},{2,10},{3,11},{4,12},{5,13},{6,14},{7,15},{8,0},{9,1},... | collective-permute-start | bytes 36872 | tf_op jit(solution)/shard_map/ppermute | solution.py:10
  145.8 2.7 collective-permute-start.14
  149.4 5.3 %collective-permute-start.34 = (bf16[75,128]{0,1:T(8,128)(2,1)S(1)}, bf16[75,128]{0,1:T(8,128)(2,1)S(1)}, u32[]{:S(2)}, u32[]{:S(2)}) collective-permute-start(bf16[75,128]{0,1:T(8,128)(2,1)S(1)} %collective-permute-done.33), channel_id=1, source_target_pairs={{0,8},{1,9},{2,10},{3,11},{4,12},{5,13},{6,14},{7,15},{8,0},{9,1},... | collective-permute-start | bytes 57608 | tf_op jit(solution)/shard_map/ppermute | solution.py:10
  155.0 4.4 collective-permute-start.17
  159.4 3.3 collective-permute-start.16
  167.4 4.1 collective-permute-start.35
  174.5 271.0 %all-reduce.5.cloned.1.call-done = (f32[9,48,75]{2,1,0:T(8,128)}, f32[9,48,48]{2,1,0:T(8,128)}) async-done(((f32[9,48,75]{2,1,0:T(8,128)}, f32[9,48,48]{2,1,0:T(8,128)}), (f32[9,48,75]{2,1,0:T(8,128)}, f32[9,48,48]{2,1,0:T(8,128)})) %all-reduce.5.cloned.1.call-update) | async-done | bytes 212560 | tf_op jit(solution)/shard_map/psum | solution.py:143
  (159 shorter events, 41.7 us)
Async XLA Ops:
  7.2 438.3 %all-reduce.5.cloned.1.call-start = ((), (), s32[]{:S(2)}) async-start(), calls=%async_computation | async-start | bytes 884736 | tf_op jit(solution)/shard_map/psum | solution.py:143
  11.8 18.5 %collective-permute-start.18 = (f32[1,48,10]{1,0,2:T(1,128)S(1)}, f32[1,48,10]{1,0,2:T(1,128)S(1)}, u32[]{:S(2)}, u32[]{:S(2)}) collective-permute-start(f32[1,48,10]{1,0,2:T(1,128)S(1)} %stack_squeeze.28), channel_id=1, source_target_pairs={{0,1},{1,2},{2,3},{3,4},{4,5},{5,6},{6,7},{7,8},{8,9},{9,10},{10,1... | collective-permute-start | bytes 5768 | tf_op jit(solution)/shard_map/ppermute | solution.py:20
  16.4 13.7 %collective-permute-start.19 = (f32[1,48,10]{1,0,2:T(1,128)S(1)}, f32[1,48,10]{1,0,2:T(1,128)S(1)}, u32[]{:S(2)}, u32[]{:S(2)}) collective-permute-start(f32[1,48,10]{1,0,2:T(1,128)S(1)} %stack_squeeze.29), channel_id=1, source_target_pairs={{1,0},{2,1},{3,2},{4,3},{5,4},{6,5},{7,6},{8,7},{9,8},{10,9},{11,1... | collective-permute-start | bytes 5768 | tf_op jit(solution)/shard_map/ppermute | solution.py:21
  22.7 9.2 %collective-permute-start.1 = (bf16[75,128]{0,1:T(8,128)(2,1)S(1)}, bf16[75,128]{0,1:T(8,128)(2,1)S(1)}, u32[]{:S(2)}, u32[]{:S(2)}) collective-permute-start(bf16[75,128]{0,1:T(8,128)(2,1)S(1)} %bitcast.327), channel_id=1, source_target_pairs={{0,1},{1,0},{2,3},{3,2},{4,5},{5,4},{6,7},{7,6},{8,9},{9,8},{10,11... | collective-permute-start | bytes 57608 | tf_op jit(solution)/shard_map/ppermute | solution.py:10
  31.9 8.4 %collective-permute-start.2 = (bf16[75,128]{0,1:T(8,128)(2,1)S(1)}, bf16[75,128]{0,1:T(8,128)(2,1)S(1)}, u32[]{:S(2)}, u32[]{:S(2)}) collective-permute-start(bf16[75,128]{0,1:T(8,128)(2,1)S(1)} %collective-permute-done.1), channel_id=1, source_target_pairs={{0,2},{1,3},{2,0},{3,1},{4,6},{5,7},{6,4},{7,5},{8,10},{9,11},{10,... | collective-permute-start | bytes 57608 | tf_op jit(solution)/shard_map/ppermute | solution.py:10
  36.9 6.6 %collective-permute-start.23 = (bf16[48,128]{1,0:T(8,128)(2,1)S(1)}, bf16[48,128]{1,0:T(8,128)(2,1)S(1)}, u32[]{:S(2)}, u32[]{:S(2)}) collective-permute-start(bf16[48,128]{1,0:T(8,128)(2,1)S(1)} %collective-permute-done.22), channel_id=1, source_target_pairs={{0,2},{1,3},{2,0},{3,1},{4,6},{5,7},{6,4},{7,5},{8,10},{9,11},{10,... | collective-permute-start | bytes 36872 | tf_op jit(solution)/shard_map/ppermute | solution.py:10
  40.3 17.9 %collective-permute-start.3 = (bf16[75,128]{0,1:T(8,128)(2,1)S(1)}, bf16[75,128]{0,1:T(8,128)(2,1)S(1)}, u32[]{:S(2)}, u32[]{:S(2)}) collective-permute-start(bf16[75,128]{0,1:T(8,128)(2,1)S(1)} %collective-permute-done.2), channel_id=1, source_target_pairs={{0,4},{1,5},{2,6},{3,7},{4,0},{5,1},{6,2},{7,3},{8,12},{9,13},{10,... | collective-permute-start | bytes 57608 | tf_op jit(solution)/shard_map/ppermute | solution.py:10
  42.2 11.7 %collective-permute-start.21 = (bf16[1,48,128]{2,1,0:T(8,128)(2,1)S(1)}, bf16[1,48,128]{2,1,0:T(8,128)(2,1)S(1)}, u32[]{:S(2)}, u32[]{:S(2)}) collective-permute-start(bf16[1,48,128]{2,1,0:T(8,128)(2,1)S(1)} %get-tuple-element.130), channel_id=1, source_target_pairs={{32,0},{64,32},{96,64},{128,96},{160,128},{192,160},{224,192},{256... | collective-permute-start | bytes 36872 | tf_op jit(solution)/shard_map/ppermute | solution.py:21
  43.5 11.8 %collective-permute-start.24 = (bf16[48,128]{1,0:T(8,128)(2,1)S(1)}, bf16[48,128]{1,0:T(8,128)(2,1)S(1)}, u32[]{:S(2)}, u32[]{:S(2)}) collective-permute-start(bf16[48,128]{1,0:T(8,128)(2,1)S(1)} %collective-permute-done.23), channel_id=1, source_target_pairs={{0,4},{1,5},{2,6},{3,7},{4,0},{5,1},{6,2},{7,3},{8,12},{9,13},{10,... | collective-permute-start | bytes 36872 | tf_op jit(solution)/shard_map/ppermute | solution.py:10
  47.8 16.8 %collective-permute-start.20 = (bf16[1,48,128]{2,1,0:T(8,128)(2,1)S(1)}, bf16[1,48,128]{2,1,0:T(8,128)(2,1)S(1)}, u32[]{:S(2)}, u32[]{:S(2)}) collective-permute-start(bf16[1,48,128]{2,1,0:T(8,128)(2,1)S(1)} %get-tuple-element.131), channel_id=1, source_target_pairs={{0,32},{32,64},{64,96},{96,128},{128,160},{160,192},{192,224},{224... | collective-permute-start | bytes 36872 | tf_op jit(solution)/shard_map/ppermute | solution.py:20
  51.8 12.8 %collective-permute-start = (bf16[75,1,128]{0,2,1:T(8,128)(2,1)S(1)}, bf16[75,1,128]{0,2,1:T(8,128)(2,1)S(1)}, u32[]{:S(2)}, u32[]{:S(2)}) collective-permute-start(bf16[75,1,128]{0,2,1:T(8,128)(2,1)S(1)} %copy.200), channel_id=1, source_target_pairs={{0,32},{32,64},{64,96},{96,128},{128,160},{160,192},{192,224},{224... | collective-permute-start | bytes 57608 | tf_op jit(solution)/shard_map/ppermute | solution.py:20
  53.9 19.2 %collective-permute-start.6 = (bf16[75,1,128]{0,2,1:T(8,128)(2,1)S(1)}, bf16[75,1,128]{0,2,1:T(8,128)(2,1)S(1)}, u32[]{:S(2)}, u32[]{:S(2)}) collective-permute-start(bf16[75,1,128]{0,2,1:T(8,128)(2,1)S(1)} %copy.201), channel_id=1, source_target_pairs={{32,0},{64,32},{96,64},{128,96},{160,128},{192,160},{224,192},{256... | collective-permute-start | bytes 57608 | tf_op jit(solution)/shard_map/ppermute | solution.py:21
  55.4 9.4 %collective-permute-start.25 = (bf16[48,128]{1,0:T(8,128)(2,1)S(1)}, bf16[48,128]{1,0:T(8,128)(2,1)S(1)}, u32[]{:S(2)}, u32[]{:S(2)}) collective-permute-start(bf16[48,128]{1,0:T(8,128)(2,1)S(1)} %collective-permute-done.24), channel_id=1, source_target_pairs={{0,8},{1,9},{2,10},{3,11},{4,12},{5,13},{6,14},{7,15},{8,0},{9,1},... | collective-permute-start | bytes 36872 | tf_op jit(solution)/shard_map/ppermute | solution.py:10
  58.1 8.8 %collective-permute-start.4 = (bf16[75,128]{0,1:T(8,128)(2,1)S(1)}, bf16[75,128]{0,1:T(8,128)(2,1)S(1)}, u32[]{:S(2)}, u32[]{:S(2)}) collective-permute-start(bf16[75,128]{0,1:T(8,128)(2,1)S(1)} %collective-permute-done.3), channel_id=1, source_target_pairs={{0,8},{1,9},{2,10},{3,11},{4,12},{5,13},{6,14},{7,15},{8,0},{9,1},... | collective-permute-start | bytes 57608 | tf_op jit(solution)/shard_map/ppermute | solution.py:10
  64.7 7.2 %collective-permute-start.26 = (bf16[48,128]{1,0:T(8,128)(2,1)S(1)}, bf16[48,128]{1,0:T(8,128)(2,1)S(1)}, u32[]{:S(2)}, u32[]{:S(2)}) collective-permute-start(bf16[48,128]{1,0:T(8,128)(2,1)S(1)} %collective-permute-done.25), channel_id=1, source_target_pairs={{0,16},{1,17},{2,18},{3,19},{4,20},{5,21},{6,22},{7,23},{8,24},{9,... | collective-permute-start | bytes 36872 | tf_op jit(solution)/shard_map/ppermute | solution.py:10
  66.9 6.2 %collective-permute-start.5 = (bf16[75,128]{0,1:T(8,128)(2,1)S(1)}, bf16[75,128]{0,1:T(8,128)(2,1)S(1)}, u32[]{:S(2)}, u32[]{:S(2)}) collective-permute-start(bf16[75,128]{0,1:T(8,128)(2,1)S(1)} %collective-permute-done.4), channel_id=1, source_target_pairs={{0,16},{1,17},{2,18},{3,19},{4,20},{5,21},{6,22},{7,23},{8,24},{9,... | collective-permute-start | bytes 57608 | tf_op jit(solution)/shard_map/ppermute | solution.py:10
  73.4 10.7 %collective-permute-start.8 = (bf16[75,10,1]{2,0,1:T(8,128)(2,1)S(1)}, bf16[75,10,1]{2,0,1:T(8,128)(2,1)S(1)}, u32[]{:S(2)}, u32[]{:S(2)}) collective-permute-start(bf16[75,10,1]{2,0,1:T(8,128)(2,1)S(1)} %get-tuple-element.134), channel_id=1, source_target_pairs={{1,0},{2,1},{3,2},{4,3},{5,4},{6,5},{7,6},{8,7},{9,8},{10,9},{11,1... | collective-permute-start | bytes 4508 | tf_op jit(solution)/shard_map/ppermute | solution.py:21
  79.5 5.8 %collective-permute-start.7 = (bf16[75,10,1]{2,0,1:T(8,128)(2,1)S(1)}, bf16[75,10,1]{2,0,1:T(8,128)(2,1)S(1)}, u32[]{:S(2)}, u32[]{:S(2)}) collective-permute-start(bf16[75,10,1]{2,0,1:T(8,128)(2,1)S(1)} %get-tuple-element.135), channel_id=1, source_target_pairs={{0,1},{1,2},{2,3},{3,4},{4,5},{5,6},{6,7},{7,8},{8,9},{9,10},{10,1... | collective-permute-start | bytes 4508 | tf_op jit(solution)/shard_map/ppermute | solution.py:20
  88.0 37.5 %collective-permute-start.9 = (bf16[48,1,128]{2,0,1:T(8,128)(2,1)S(1)}, bf16[48,1,128]{2,0,1:T(8,128)(2,1)S(1)}, u32[]{:S(2)}, u32[]{:S(2)}) collective-permute-start(bf16[48,1,128]{2,0,1:T(8,128)(2,1)S(1)} %get-tuple-element.144), channel_id=1, source_target_pairs={{0,32},{32,64},{64,96},{96,128},{128,160},{160,192},{192,224},{224... | collective-permute-start | bytes 36872 | tf_op jit(solution)/shard_map/ppermute | solution.py:20
  92.5 21.6 %collective-permute-start.10 = (bf16[48,128]{1,0:T(8,128)(2,1)S(1)}, bf16[48,128]{1,0:T(8,128)(2,1)S(1)}, u32[]{:S(2)}, u32[]{:S(2)}) collective-permute-start(bf16[48,128]{1,0:T(8,128)(2,1)S(1)} %get-tuple-element.145), channel_id=1, source_target_pairs={{0,1},{1,0},{2,3},{3,2},{4,5},{5,4},{6,7},{7,6},{8,9},{9,8},{10,11... | collective-permute-start | bytes 36872 | tf_op jit(solution)/shard_map/ppermute | solution.py:10
  100.2 54.6 %collective-permute-start.15 = (bf16[48,1,128]{2,0,1:T(8,128)(2,1)S(1)}, bf16[48,1,128]{2,0,1:T(8,128)(2,1)S(1)}, u32[]{:S(2)}, u32[]{:S(2)}) collective-permute-start(bf16[48,1,128]{2,0,1:T(8,128)(2,1)S(1)} %get-tuple-element.146), channel_id=1, source_target_pairs={{32,0},{64,32},{96,64},{128,96},{160,128},{192,160},{224,192},{256... | collective-permute-start | bytes 36872 | tf_op jit(solution)/shard_map/ppermute | solution.py:21
  114.1 7.2 %collective-permute-start.11 = (bf16[48,128]{1,0:T(8,128)(2,1)S(1)}, bf16[48,128]{1,0:T(8,128)(2,1)S(1)}, u32[]{:S(2)}, u32[]{:S(2)}) collective-permute-start(bf16[48,128]{1,0:T(8,128)(2,1)S(1)} %collective-permute-done.10), channel_id=1, source_target_pairs={{0,2},{1,3},{2,0},{3,1},{4,6},{5,7},{6,4},{7,5},{8,10},{9,11},{10,... | collective-permute-start | bytes 36872 | tf_op jit(solution)/shard_map/ppermute | solution.py:10
  116.1 15.5 %collective-permute-start.31 = (bf16[75,128]{0,1:T(8,128)(2,1)S(1)}, bf16[75,128]{0,1:T(8,128)(2,1)S(1)}, u32[]{:S(2)}, u32[]{:S(2)}) collective-permute-start(bf16[75,128]{0,1:T(8,128)(2,1)S(1)} %get-tuple-element.126), channel_id=1, source_target_pairs={{0,1},{1,0},{2,3},{3,2},{4,5},{5,4},{6,7},{7,6},{8,9},{9,8},{10,11... | collective-permute-start | bytes 57608 | tf_op jit(solution)/shard_map/ppermute | solution.py:10
  121.4 13.9 %collective-permute-start.12 = (bf16[48,128]{1,0:T(8,128)(2,1)S(1)}, bf16[48,128]{1,0:T(8,128)(2,1)S(1)}, u32[]{:S(2)}, u32[]{:S(2)}) collective-permute-start(bf16[48,128]{1,0:T(8,128)(2,1)S(1)} %collective-permute-done.11), channel_id=1, source_target_pairs={{0,4},{1,5},{2,6},{3,7},{4,0},{5,1},{6,2},{7,3},{8,12},{9,13},{10,... | collective-permute-start | bytes 36872 | tf_op jit(solution)/shard_map/ppermute | solution.py:10
  124.2 24.2 %collective-permute-start.30 = (bf16[1,75,128]{1,2,0:T(8,128)(2,1)S(1)}, bf16[1,75,128]{1,2,0:T(8,128)(2,1)S(1)}, u32[]{:S(2)}, u32[]{:S(2)}) collective-permute-start(bf16[1,75,128]{1,2,0:T(8,128)(2,1)S(1)} %get-tuple-element.127), channel_id=1, source_target_pairs={{32,0},{64,32},{96,64},{128,96},{160,128},{192,160},{224,192},{256... | collective-permute-start | bytes 57608 | tf_op jit(solution)/shard_map/ppermute | solution.py:21
  125.5 22.9 %collective-permute-start.29 = (bf16[1,75,128]{1,2,0:T(8,128)(2,1)S(1)}, bf16[1,75,128]{1,2,0:T(8,128)(2,1)S(1)}, u32[]{:S(2)}, u32[]{:S(2)}) collective-permute-start(bf16[1,75,128]{1,2,0:T(8,128)(2,1)S(1)} %get-tuple-element.128), channel_id=1, source_target_pairs={{0,32},{32,64},{64,96},{96,128},{128,160},{160,192},{192,224},{224... | collective-permute-start | bytes 57608 | tf_op jit(solution)/shard_map/ppermute | solution.py:20
  131.6 12.3 %collective-permute-start.32 = (bf16[75,128]{0,1:T(8,128)(2,1)S(1)}, bf16[75,128]{0,1:T(8,128)(2,1)S(1)}, u32[]{:S(2)}, u32[]{:S(2)}) collective-permute-start(bf16[75,128]{0,1:T(8,128)(2,1)S(1)} %collective-permute-done.31), channel_id=1, source_target_pairs={{0,2},{1,3},{2,0},{3,1},{4,6},{5,7},{6,4},{7,5},{8,10},{9,11},{10,... | collective-permute-start | bytes 57608 | tf_op jit(solution)/shard_map/ppermute | solution.py:10
  135.3 10.5 %collective-permute-start.13 = (bf16[48,128]{1,0:T(8,128)(2,1)S(1)}, bf16[48,128]{1,0:T(8,128)(2,1)S(1)}, u32[]{:S(2)}, u32[]{:S(2)}) collective-permute-start(bf16[48,128]{1,0:T(8,128)(2,1)S(1)} %collective-permute-done.12), channel_id=1, source_target_pairs={{0,8},{1,9},{2,10},{3,11},{4,12},{5,13},{6,14},{7,15},{8,0},{9,1},... | collective-permute-start | bytes 36872 | tf_op jit(solution)/shard_map/ppermute | solution.py:10
  145.8 9.0 %collective-permute-start.14 = (bf16[48,128]{1,0:T(8,128)(2,1)S(1)}, bf16[48,128]{1,0:T(8,128)(2,1)S(1)}, u32[]{:S(2)}, u32[]{:S(2)}) collective-permute-start(bf16[48,128]{1,0:T(8,128)(2,1)S(1)} %collective-permute-done.13), channel_id=1, source_target_pairs={{0,16},{1,17},{2,18},{3,19},{4,20},{5,21},{6,22},{7,23},{8,24},{9,... | collective-permute-start | bytes 36872 | tf_op jit(solution)/shard_map/ppermute | solution.py:10
  149.4 17.9 %collective-permute-start.34 = (bf16[75,128]{0,1:T(8,128)(2,1)S(1)}, bf16[75,128]{0,1:T(8,128)(2,1)S(1)}, u32[]{:S(2)}, u32[]{:S(2)}) collective-permute-start(bf16[75,128]{0,1:T(8,128)(2,1)S(1)} %collective-permute-done.33), channel_id=1, source_target_pairs={{0,8},{1,9},{2,10},{3,11},{4,12},{5,13},{6,14},{7,15},{8,0},{9,1},... | collective-permute-start | bytes 57608 | tf_op jit(solution)/shard_map/ppermute | solution.py:10
  155.0 8.3 %collective-permute-start.17 = (bf16[48,10,1]{2,0,1:T(8,128)(2,1)S(1)}, bf16[48,10,1]{2,0,1:T(8,128)(2,1)S(1)}, u32[]{:S(2)}, u32[]{:S(2)}) collective-permute-start(bf16[48,10,1]{2,0,1:T(8,128)(2,1)S(1)} %get-tuple-element.142), channel_id=1, source_target_pairs={{1,0},{2,1},{3,2},{4,3},{5,4},{6,5},{7,6},{8,7},{9,8},{10,9},{11,1... | collective-permute-start | bytes 2888 | tf_op jit(solution)/shard_map/ppermute | solution.py:21
  167.4 6.2 %collective-permute-start.35 = (bf16[75,128]{0,1:T(8,128)(2,1)S(1)}, bf16[75,128]{0,1:T(8,128)(2,1)S(1)}, u32[]{:S(2)}, u32[]{:S(2)}) collective-permute-start(bf16[75,128]{0,1:T(8,128)(2,1)S(1)} %collective-permute-done.34), channel_id=1, source_target_pairs={{0,16},{1,17},{2,18},{3,19},{4,20},{5,21},{6,22},{7,23},{8,24},{9,... | collective-permute-start | bytes 57608 | tf_op jit(solution)/shard_map/ppermute | solution.py:10
  (11 other events, 57.3 us)
Sparse Core Ops, SparseCore 0:
  172.6 272.8 all-reduce.4
where the time goes:
time: 456 us; the launch traced here: 455 us
  waiting for transfers between devices  283 us (62%)
  starting transfers between devices  133 us (29%)
  between operations  15.3 us (3%)
  matrix products  13.4 us (3%)
  local copies, waits for them, and re-layouts  5.33 us (1%)
  other arithmetic  4.94 us (1%)
    psum x1, waiting for transfers between devices, body(): grad_w1, grad_w2 = lax.psum((term_w1, term_w2), ('lat', 'lon'))  271 us
    ppermute x20, starting transfers between devices, from_partner(): lax.ppermute(x, axis, [(i, i ^ 1 << bit) for i in range(lax.axis_size(axi...  79.5 us
    ppermute x8, starting transfers between devices, extended(): before = lax.ppermute(last, axis, up)  29.3 us
    ppermute x8, starting transfers between devices, extended(): after = lax.ppermute(leading, axis, down)  24.3 us
  transfers between devices with their start and end apart: 37, of which 11 were waited for; matrix products, arithmetic and copies ran while one was open for 3% of the time, Pallas kernels for 0%

commit v1 on v0

v1 whole, which is shorter than its diff:
```python
import functools
import math

import jax
import jax.numpy as jnp
from jax import lax
from jax.experimental import pallas as pl
from jax.experimental.pallas import tpu as pltpu
from jax.sharding import PartitionSpec as P

MESH = pl.DeviceIdType.MESH
BF = jnp.bfloat16
F32 = jnp.float32
CIN, CH, KX = 75, 48, 80
ROWS, LANES = 8, 128
EXT = ROWS + 4
RIM = ROWS + 2
TILES = 27


def nn(a, b):
    return lax.dot_general(a, b, (((1,), (0,)), ((), ())), preferred_element_type=F32)


def nt(a, b):
    return lax.dot_general(a, b, (((1,), (1,)), ((), ())), preferred_element_type=F32)


def tn(a, b):
    return lax.dot_general(a, b, (((0,), (0,)), ((), ())), preferred_element_type=F32)


def gelu_parts(a):
    coeff = 0.7978845608
    inner = coeff * (a + 0.044715 * a * a * a)
    tval = jnp.tanh(inner)
    value = 0.5 * a * (1.0 + tval)
    slope = 0.5 * (1.0 + tval) + 0.5 * a * (1.0 - tval * tval) * coeff * (1.0 + 0.134145 * a * a)
    return (value, slope)


def tile(r, count=1):
    return slice(r * LANES, (r + count) * LANES)


def gather_rows(y, rows):
    n = rows * LANES
    c = y.shape[0] // 3
    return y[:c, :n] + y[c : 2 * c, LANES : LANES + n] + y[2 * c :, 2 * LANES : 2 * LANES + n]


def kernel(
    nlat, nlon, per, owners,
    f_ref, wa1, wa1n, wa2, tb2, tb2n, tb1, tb1n,
    out_ref, dx_ref, dw_ref,
    xm, xg, packs, mine, d1m, d1g, d2m, d2g, hd, dad, am, ae, gbuf, rbuf1, rbuf2, obuf,
    send_sem, recv_sem, red_send, red_recv,
):
    lat, lon = lax.axis_index("lat"), lax.axis_index("lon")
    top, bottom = lat == nlat - 1, lat == 0
    east, west = lax.rem(lon + 1, nlon), lax.rem(lon + nlon - 1, nlon)

    barrier = pltpu.get_barrier_semaphore()

    def greet(a, b):
        pl.semaphore_signal(barrier, inc=1, device_id=(a, b), device_id_type=MESH)

    @pl.loop(1, nlon)
    def _(j):
        greet(lat, lax.rem(lon + j, nlon))

    @pl.loop(1, nlat)
    def _(j):
        greet(lax.rem(lat + j, nlat), lon)

    @pl.when(jnp.logical_not(top))
    def _():
        greet(lat + 1, east)
        greet(lat + 1, west)

    @pl.when(jnp.logical_not(bottom))
    def _():
        greet(lat - 1, east)
        greet(lat - 1, west)

    cell = lax.broadcasted_iota(jnp.int32, (32, ROWS * LANES), 0)
    place = lax.broadcasted_iota(jnp.int32, (32, ROWS * LANES), 1)
    want = ((cell % 16) // 2) * LANES + cell % 2 + jnp.where(cell < 16, LANES - 2, 0)
    picked = nt((place == want).astype(F32).astype(BF), f_ref[...]).astype(BF)
    mine[0] = picked[:16]
    mine[1] = picked[16:]

    pl.semaphore_wait(
        barrier,
        nlon - 1 + nlat - 1 + jnp.where(top, 0, 2) + jnp.where(bottom, 0, 2),
    )

    def send(src, dst, slot, a, b):
        return pltpu.make_async_remote_copy(
            src_ref=src, dst_ref=dst, send_sem=send_sem.at[slot], recv_sem=recv_sem.at[slot],
            device_id=(a, b), device_id_type=MESH,
        )

    low, high = f_ref.at[:, tile(0, 2)], f_ref.at[:, tile(ROWS - 2, 2)]
    above, below = xm.at[:, tile(ROWS + 2, 2)], xm.at[:, tile(0, 2)]
    fold_e = lax.rem(2 * nlon - 2 - lon, nlon)
    fold_w = lax.rem(nlon - lon, nlon)

    @pl.when(jnp.logical_not(top))
    def _():
        send(high, below, 7, lat + 1, lon).start()

    @pl.when(top)
    def _():
        send(high, above, 6, lat, nlon - 1 - lon).start()

    @pl.when(jnp.logical_not(bottom))
    def _():
        send(low, above, 8, lat - 1, lon).start()

    send(mine.at[0], packs.at[0], 0, lat, east).start()
    send(mine.at[1], packs.at[1], 1, lat, west).start()

    @pl.when(jnp.logical_not(bottom))
    def _():
        send(mine.at[0], packs.at[2], 2, lat - 1, east).start()
        send(mine.at[1], packs.at[3], 3, lat - 1, west).start()

    @pl.when(jnp.logical_not(top))
    def _():
        send(mine.at[0], packs.at[4], 4, lat + 1, east).start()
        send(mine.at[1], packs.at[5], 5, lat + 1, west).start()

    @pl.when(top)
    def _():
        @pl.when(fold_e != lon)
        def _():
            send(mine.at[0], packs.at[3], 9, lat, fold_e).start()

        @pl.when(fold_w != lon)
        def _():
            send(mine.at[1], packs.at[2], 10, lat, fold_w).start()

        @pl.when(fold_e == lon)
        def _():
            packs[3] = mine[0]

        @pl.when(fold_w == lon)
        def _():
            packs[2] = mine[1]

    @pl.when(bottom)
    def _():
        xm[:, tile(0, 2)] = jnp.zeros((128, 2 * LANES), BF)
        packs[4] = jnp.zeros((16, 128), BF)
        packs[5] = jnp.zeros((16, 128), BF)

    xm[:, tile(2, ROWS)] = f_ref[...]
    zero = jnp.zeros((CH, LANES), BF)
    for dr in range(3):
        at = slice(dr * CH, (dr + 1) * CH)
        ae[at, tile(dr, ROWS)] = f_ref[KX:, :]
        for r in range(RIM):
            if not dr <= r < dr + ROWS:
                am[at, tile(r)] = zero
                ae[at, tile(r)] = zero

    k = lax.broadcasted_iota(jnp.int32, (96, 1), 0)
    slot, row, j = k // 16, (k % 16) // 2, k % 2
    row_to = jnp.where(slot < 2, row + 2, jnp.where(slot < 4, row + 10, row - 6))
    row_to = jnp.where((slot >= 2) & (slot < 4) & top, 17 - row, row_to)
    lane_to = jnp.where(slot % 2 == 0, LANES - 2 + j, j)
    lane_to = jnp.where((slot == 2) & top, LANES - 1 - j, lane_to)
    lane_to = jnp.where((slot == 3) & top, 1 - j, lane_to)
    good = (slot < 2) | ((slot < 4) & (row_to < EXT)) | ((slot >= 4) & (row_to >= 0))
    goal = jnp.where(good, row_to * LANES + lane_to, -1)

    def landed(ref, slot):
        pltpu.make_async_copy(ref, ref, recv_sem.at[slot]).wait()

    landed(packs.at[0], 0)
    landed(packs.at[1], 1)

    @pl.when(jnp.logical_not(top))
    def _():
        landed(above, 8)
        landed(packs.at[2], 2)
        landed(packs.at[3], 3)

    @pl.when(top)
    def _():
        landed(above, 6)

        @pl.when(fold_e != lon)
        def _():
            landed(packs.at[3], 9)

        @pl.when(fold_w != lon)
        def _():
            landed(packs.at[2], 10)

        back = lax.broadcasted_iota(jnp.int32, (LANES, LANES), 0)
        back = back + lax.broadcasted_iota(jnp.int32, (LANES, LANES), 1)
        back = (back == LANES - 1).astype(F32).astype(BF)
        first = nn(xm[:, tile(ROWS + 2)], back).astype(BF)
        second = nn(xm[:, tile(ROWS + 3)], back).astype(BF)
        xm[:, tile(ROWS + 2)] = second
        xm[:, tile(ROWS + 3)] = first

    @pl.when(jnp.logical_not(bottom))
    def _():
        landed(below, 7)
        landed(packs.at[4], 4)
        landed(packs.at[5], 5)

    flat = jnp.concatenate([packs[s] for s in range(6)], axis=0)
    lanes96 = lax.broadcasted_iota(jnp.int32, (96, EXT * LANES), 1)
    xg[...] = tn(flat, (lanes96 == goal).astype(F32).astype(BF)).astype(BF)

    lane = lax.broadcasted_iota(jnp.int32, (1, LANES), 1)

    def shifts(main, ghost):
        main, ghost = main.astype(F32), ghost.astype(F32)
        left = (pltpu.roll(main, 1, 1), pltpu.roll(ghost, 1, 1))
        right = (pltpu.roll(main, LANES - 1, 1), pltpu.roll(ghost, LANES - 1, 1))
        a = jnp.where(lane == 0, left[1], left[0]).astype(BF)
        b = jnp.where(lane == LANES - 1, right[1], right[0]).astype(BF)
        ga = jnp.where(lane == 0, left[0], left[1]).astype(BF)
        gb = jnp.where(lane == LANES - 1, right[0], right[1]).astype(BF)
        return a, b, ga, gb

    for r in range(EXT):
        t = tile(r)
        main, ghost = xm[:, t], xg[:, t]
        a, b, ga, gb = shifts(main, ghost)
        for q, m, g in ((0, a, ga), (1, main, ghost), (2, b, gb)):
            d1m[q * KX : (q + 1) * KX, t] = m[:KX]
            d1g[q * KX : (q + 1) * KX, t] = g[:KX]
            d2m[q * CH : (q + 1) * CH, t] = m[KX:]
            d2g[q * CH : (q + 1) * CH, t] = g[KX:]

    def hidden(d1, d2, field):
        a = gather_rows(nn(wa1[...], d1[...]), RIM)
        last = gather_rows(nn(wa1n[...], d1[:, tile(RIM - 1, 3)]), 1)
        a = jnp.concatenate([a[:, : (RIM - 1) * LANES], last], axis=1)
        value, slope = gelu_parts(a)
        sea = field[CIN : CIN + 1, tile(1, RIM)].astype(F32)
        z = jnp.concatenate(
            [nn(tb2[...], d2[:, tile(0, RIM)]), nn(tb2n[...], d2[:, tile(RIM, 2)])], axis=1
        )
        grad = (gather_rows(z, RIM) * (slope * sea)).astype(BF)
        return (value * sea).astype(BF), grad

    hm, gm = hidden(d1m, d2m, xm)
    hg, gg = hidden(d1g, d2g, xg)
    for dr in range(3):
        am[dr * CH : (dr + 1) * CH, tile(dr, ROWS)] = gm[:, tile(1, ROWS)]
    for r in range(RIM):
        t = tile(r)
        for ref, main, ghost in ((hd, hm[:, t], hg[:, t]), (dad, gm[:, t], gg[:, t])):
            a, b, _, _ = shifts(main, ghost)
            ref[0:CH, t] = a
            ref[CH : 2 * CH, t] = main
            ref[2 * CH :, t] = b

    term2 = nt(ae[...], hd[...])
    term1 = nt(am[...], d1m[:, tile(1, RIM)])
    terms = jnp.concatenate([term1, term2], axis=1).astype(BF)
    for t in range(TILES):
        a, b = t // 3, t % 3
        gbuf[t // per, (t % per) * 16 : (t % per + 1) * 16, :] = terms[16 * a : 16 * a + 16, tile(b)]
    if TILES < per * owners:
        gbuf[owners - 1, (TILES - per * (owners - 1)) * 16 :, :] = jnp.zeros(
            ((per * owners - TILES) * 16, LANES), BF
        )

    def reduce_send(src, dst, phase, a, b):
        return pltpu.make_async_remote_copy(
            src_ref=src, dst_ref=dst, send_sem=red_send.at[phase], recv_sem=red_recv.at[phase],
            device_id=(a, b), device_id_type=MESH,
        )

    @pl.loop(1, nlon)
    def _(j):
        peer = lax.rem(lon + j, nlon)

        @pl.when(peer < owners)
        def _():
            reduce_send(gbuf.at[peer], rbuf1.at[lon], 0, lat, peer).start()

    sea = f_ref[CIN : CIN + 1, :].astype(F32)
    out_ref[...] = (gather_rows(nn(wa2[...], hd[...]), ROWS) * sea).astype(BF)
    v = jnp.concatenate(
        [nn(tb1[...], dad[:, tile(0, RIM - 1)]), nn(tb1n[...], dad[:, tile(RIM - 1)])], axis=1
    )
    dx_ref[...] = gather_rows(v, ROWS).astype(BF)

    owner = lon < owners

    @pl.when(owner)
    def _():
        rbuf1[lon] = gbuf[lon]
        some = rbuf1.at[pl.ds(0, nlon - 1)]
        pltpu.make_async_copy(some, some, red_recv.at[0]).wait()
        rbuf2[lat] = jnp.sum(rbuf1[...].astype(F32), axis=0).astype(BF)

        @pl.loop(1, nlat)
        def _(j):
            peer = lax.rem(lat + j, nlat)
            reduce_send(rbuf2.at[lat], rbuf2.at[lat], 1, peer, lon).start()

        some2 = rbuf2.at[pl.ds(0, nlat - 1)]
        pltpu.make_async_copy(some2, some2, red_recv.at[1]).wait()
        obuf[lon] = jnp.sum(rbuf2[...].astype(F32), axis=0).astype(BF)

        @pl.loop(1, nlon)
        def _(j):
            peer = lax.rem(lon + j, nlon)
            reduce_send(obuf.at[lon], obuf.at[lon], 2, lat, peer).start()

        got = obuf.at[pl.ds(0, owners - 1)]
        pltpu.make_async_copy(got, got, red_recv.at[2]).wait()

    @pl.when(jnp.logical_not(owner))
    def _():
        pltpu.make_async_copy(obuf, obuf, red_recv.at[2]).wait()

    dw_ref[...] = obuf[...]

    def sent(ref, sem):
        pltpu.make_async_copy(ref, ref, sem).wait()

    sent(mine.at[0], send_sem.at[0])
    sent(mine.at[1], send_sem.at[1])

    @pl.when(jnp.logical_not(top))
    def _():
        sent(high, send_sem.at[7])
        sent(mine.at[0], send_sem.at[4])
        sent(mine.at[1], send_sem.at[5])

    @pl.when(top)
    def _():
        sent(high, send_sem.at[6])

        @pl.when(fold_e != lon)
        def _():
            sent(mine.at[0], send_sem.at[9])

        @pl.when(fold_w != lon)
        def _():
            sent(mine.at[1], send_sem.at[10])

    @pl.when(jnp.logical_not(bottom))
    def _():
        sent(low, send_sem.at[8])
        sent(mine.at[0], send_sem.at[2])
        sent(mine.at[1], send_sem.at[3])

    @pl.when(owner)
    def _():
        sent(gbuf.at[pl.ds(0, owners - 1)], red_send.at[0])
        sent(rbuf2.at[pl.ds(0, nlat - 1)], red_send.at[1])
        sent(rbuf1.at[pl.ds(0, nlon - 1)], red_send.at[2])

    @pl.when(jnp.logical_not(owner))
    def _():
        sent(gbuf, red_send.at[0])


def stacked(w, pad):
    w = jnp.pad(w, ((0, 0), (0, 0), (0, 0), (0, pad)))
    return w.transpose(0, 2, 1, 3).reshape(3 * w.shape[2], 3 * w.shape[3])


def body(nlat, nlon, fields, mask, w1, w2, cotangent):
    sea = mask.astype(BF)[None]
    field = jnp.concatenate(
        [fields, sea, jnp.zeros((KX - CIN - 1, ROWS, LANES), BF), cotangent * sea], axis=0
    ).reshape(KX + CH, ROWS * LANES)
    top = lax.axis_index("lat") == nlat - 1
    k1 = w1.reshape(3, 3, CH, CIN)
    k2 = w2.reshape(3, 3, CH, CH)
    k1r, k2r = k1[::-1, ::-1], k2[::-1, ::-1]
    swap = (0, 1, 3, 2)
    rows = ((0, 0), (0, 0), (0, KX - CIN), (0, 0))
    wa1 = stacked(k1, KX - CIN)
    wa1n = stacked(jnp.where(top, k1r, k1), KX - CIN)
    wa2 = stacked(k2, 0)
    tb2 = stacked(k2r.transpose(swap), 0)
    tb2n = stacked(jnp.where(top, k2, k2r).transpose(swap), 0)
    tb1 = stacked(jnp.pad(k1r.transpose(swap), rows), 0)
    tb1n = stacked(jnp.pad(jnp.where(top, k1, k1r).transpose(swap), rows), 0)

    per = -(-TILES // nlon)
    owners = -(-TILES // per)
    chunk = (per * 16, LANES)
    wide, slim = EXT * LANES, RIM * LANES
    vm = pl.BlockSpec(memory_space=pltpu.VMEM)
    out, dx, dw = pl.pallas_call(
        functools.partial(kernel, nlat, nlon, per, owners),
        out_shape=(
            jax.ShapeDtypeStruct((CH, ROWS * LANES), BF),
            jax.ShapeDtypeStruct((KX, ROWS * LANES), BF),
            jax.ShapeDtypeStruct((owners,) + chunk, BF),
        ),
        in_specs=[vm] * 8,
        out_specs=(vm, vm, vm),
        scratch_shapes=[
            pltpu.VMEM((128, wide), BF),
            pltpu.VMEM((128, wide), BF),
            pltpu.VMEM((6, 16, 128), BF),
            pltpu.VMEM((2, 16, 128), BF),
            pltpu.VMEM((3 * KX, wide), BF),
            pltpu.VMEM((3 * KX, wide), BF),
            pltpu.VMEM((3 * CH, wide), BF),
            pltpu.VMEM((3 * CH, wide), BF),
            pltpu.VMEM((3 * CH, slim), BF),
            pltpu.VMEM((3 * CH, slim), BF),
            pltpu.VMEM((3 * CH, slim), BF),
            pltpu.VMEM((3 * CH, slim), BF),
            pltpu.VMEM((owners,) + chunk, BF),
            pltpu.VMEM((nlon,) + chunk, BF),
            pltpu.VMEM((nlat,) + chunk, BF),
            pltpu.VMEM((owners,) + chunk, BF),
            pltpu.SemaphoreType.DMA((11,)),
            pltpu.SemaphoreType.DMA((11,)),
            pltpu.SemaphoreType.DMA((3,)),
            pltpu.SemaphoreType.DMA((3,)),
        ],
        compiler_params=pltpu.CompilerParams(
            collective_id=0, has_side_effects=True, vmem_limit_bytes=40 * 1024 * 1024
        ),
    )(field, wa1, wa1n, wa2, tb2, tb2n, tb1, tb1n)

    factor = 1.0 / math.sqrt(ROWS * LANES * nlat * nlon)
    grads = dw.reshape(-1, 16, LANES)[:TILES].reshape(9, 3, 16, LANES).transpose(0, 2, 1, 3)
    grads = grads.reshape(3 * CH, 3 * LANES).astype(F32) * factor
    dw1 = grads[:, : 3 * KX].reshape(3, CH, 3, KX)[..., :CIN].transpose(0, 2, 1, 3)
    dw2 = grads[:, 3 * KX :].reshape(3, CH, 3, CH).transpose(0, 2, 1, 3)
    return (
        out.reshape(CH, ROWS, LANES),
        dx[:CIN].reshape(CIN, ROWS, LANES),
        dw1.reshape(9, CH, CIN),
        dw2.reshape(9, CH, CH),
    )


def solution(mesh):
    in_specs = (P(None, "lat", "lon"), P("lat", "lon"), P(), P(), P(None, "lat", "lon"))
    out_specs = (P(None, "lat", "lon"), P(None, "lat", "lon"), P(), P())
    run = functools.partial(body, mesh.shape["lat"], mesh.shape["lon"])
    return jax.shard_map(run, mesh=mesh, in_specs=in_specs, out_specs=out_specs, check_vma=False)
```

time: 456 us -> 55.1 us (0.12)
  waiting for transfers between devices: 283 us -> 0 us
  starting transfers between devices: 133 us -> 0 us
  Pallas kernels: 0 us -> 42.7 us
  between operations: 15.3 us -> 0.95 us
  matrix products: 13.4 us -> 0 us
  local copies, waits for them, and re-layouts: 5.33 us -> 9.98 us
    psum x1 -> x0, waiting for transfers between devices: 271 us -> none  [body(): grad_w1, grad_w2 = lax.psum((term_w1, term_w2), ('lat', 'lon'))]
    ppermute x36 -> x0, starting transfers between devices: 133 us -> none  [the longest x20 79.5 us: from_partner(): lax.ppermute(x, axis, [(i, i ^ 1 << bit) for i in range(lax.axis_size(axi...]
    pallas_call x0 -> x1, Pallas kernels: none -> 42.7 us  [body(): pl.pallas_call(functools.partial(kernel, nlat, nlon, per, owners), out_sh...]
    dot_general x54 -> x0, matrix products: 13.4 us -> none  [the longest x18 6.72 us: tconv(): jnp.einsum('oi,ohw->ihw', kernel[tap], wide[:, 2 - drow:4 - drow + rows_n...]
    ppermute x36 -> x0, waiting for transfers between devices: 11.6 us -> none  [the longest x8 4.71 us: extended(): after = lax.ppermute(leading, axis, down)]
  transfers between devices with their start and end apart: 37 -> 0, of which waited for: 11 -> 0; matrix products, arithmetic and copies ran while one was open for 3% -> 0% of each run, Pallas kernels for 0% -> 0%
where the time goes in v1:
time: 55.1 us; the launch traced here: 54.9 us
  Pallas kernels  42.7 us (77%)
  local copies, waits for them, and re-layouts  9.98 us (18%)
  other arithmetic  1.27 us (2%)
  between operations  0.95 us (2%)
    pallas_call x1, Pallas kernels, body(): pl.pallas_call(functools.partial(kernel, nlat, nlon, per, owners), out_sh...  42.7 us
    unnamed x15, local copies, waits for them, and re-layouts  3.77 us
    rev x2, local copies, waits for them, and re-layouts, body(): k1r, k2r = (k1[::-1, ::-1], k2[::-1, ::-1])  1.64 us

profile of v1, /device:TPU:1, one launch (start us, length us, event | category | flops | bytes accessed | tf_op | source)
XLA Modules:
  0.0 54.9 jit_solution(1367242979917831899)
XLA Ops:
  0.7 0.6 %copy-done.3 = s32[8,128]{1,0:T(8,128)S(1)} copy-done((s32[8,128]{1,0:T(8,128)S(1)}, s32[8,128]{1,0:T(8,128)}, u32[]{:S(2)}) %copy-start.3) | copy-done | bytes 4120
  1.3 0.9 %broadcast_multiply_fusion = bf16[48,8,128]{2,1,0:T(8,128)(2,1)S(1)} fusion(bf16[48,8,128]{2,1,0:T(8,128)(2,1)} %param.9, bf16[8,128]{1,0:T(8,128)(2,1)S(1)} %convert_element_type.15), kind=kLoop, calls=%fused_computation.13 | loop fusion | flops 49152 | bytes 198656 | tf_op jit(solution)/shard_map/mul | solution.py:379
  2.3 0.9 %copy-done.1 = bf16[9,48,48]{2,1,0:T(8,128)(2,1)S(1)} copy-done((bf16[9,48,48]{2,1,0:T(8,128)(2,1)S(1)}, bf16[9,48,48]{2,1,0:T(8,128)(2,1)}, u32[]{:S(2)}) %copy-start.1) | copy-done | bytes 41496
  3.2 0.1 copy.33
  3.3 0.8 %rev.7 = bf16[3,3,48,48]{2,1,3,0:T(4,128)(2,1)S(1)} reverse(bf16[3,3,48,48]{2,1,3,0:T(4,128)(2,1)S(1)} %copy.33), dimensions={0,1} | reverse | bytes 82944 | tf_op jit(solution)/shard_map/rev | solution.py:384
  4.2 0.1 reshape.74.tb2n
  4.4 0.1 reshape.73.tb2
  4.5 0.8 %copy-done = bf16[9,48,75]{2,1,0:T(8,128)(2,1)S(1)} copy-done((bf16[9,48,75]{2,1,0:T(8,128)(2,1)S(1)}, bf16[9,48,75]{2,1,0:T(8,128)(2,1)}, u32[]{:S(2)}) %copy-start) | copy-done | bytes 64824
  5.3 0.8 %rev.6 = bf16[3,3,48,75]{3,0,2,1:T(4,128)(2,1)S(1)} reverse(bf16[3,3,48,75]{3,0,2,1:T(4,128)(2,1)S(1)} %copy.29), dimensions={0,1} | reverse | bytes 129600 | tf_op jit(solution)/shard_map/rev | solution.py:384
  6.1 0.1 pad_bitcast_fusion.1
  6.2 0.1 reshape.75
  6.4 0.1 copy.36.tb1
  6.5 0.1 pad_bitcast_fusion.3
  6.6 0.1 reshape.69.wa1
  6.7 0.1 select_bitcast_fusion
  7.0 0.1 reshape.76
  7.1 0.1 copy.37.tb1n
  7.2 0.1 pad_bitcast_fusion.2
  7.3 0.1 copy.31
  7.4 0.1 reshape.70.wa1n
  7.6 0.1 reshape.72.wa2
  7.8 0.8 %copy-done.2 = bf16[75,8,128]{2,1,0:T(8,128)(2,1)S(1)} copy-done((bf16[75,8,128]{2,1,0:T(8,128)(2,1)S(1)}, bf16[75,8,128]{2,1,0:T(8,128)(2,1)}, u32[]{:S(2)}) %copy-start.2) | copy-done | bytes 153624
  8.6 0.1 pad_maximum_fusion.f_ref
  8.7 42.7 %shard_map.84 = (bf16[48,1024]{1,0:T(8,128)(2,1)S(1)}, bf16[80,1024]{1,0:T(8,128)(2,1)S(1)}, bf16[27,16,128]{2,1,0:T(8,128)(2,1)S(1)}) custom-call(bf16[128,1024]{1,0:T(8,128)(2,1)S(1)} %pad_maximum_fusion.f_ref, bf16[144,240]{1,0:T(8,128)(2,1)S(1)} %reshape.69.wa1, bf16[144,240]{1,0:T(8,128)(2,1)S(1)} %reshape.70.wa1n, bf16[144,144]{1,0:T(8,128)(2,1)S(1)} %reshape.72.wa2, ...), custom_call_target="tpu_custom_call" | custom-call | tf_op jit(solution)/shard_map/pallas_call | solution.py:400
  51.4 0.7 %copy.44 = bf16[6,8,8,128]{3,2,1,0:T(8,128)(2,1)} copy(bf16[6,8,8,128]{3,1,2,0:T(8,128)(2,1)S(1)} %bitcast.55) | data formatting | bytes 196608
  52.1 0.7 %slice.19 = bf16[75,8,128]{2,1,0:T(8,128)(2,1)} slice(bf16[80,8,128]{2,1,0:T(8,128)(2,1)S(1)} %bitcast.68), slice={[0:75], [0:8], [0:128]} | slice | bytes 307200 | tf_op jit(solution)/shard_map/reshape | solution.py:443
  52.8 0.1 copy.38
  52.9 0.1 slice.18
  53.0 0.2 reshape.79
  53.3 0.7 %copy.39 = f32[3,3,48,75]{3,2,1,0:T(8,128)} copy(f32[3,3,48,75]{3,1,2,0:T(4,128)S(1)} %slice_bitcast_fusion) | data formatting | bytes 259200 | tf_op jit(solution)/shard_map/transpose | solution.py:439
  54.0 0.2 reshape.81
  54.2 0.7 %copy.40 = f32[3,3,48,48]{3,2,1,0:T(8,128)} copy(f32[3,3,48,48]{3,1,2,0:T(4,128)S(1)} %bitcast.60) | data formatting | bytes 165888 | tf_op jit(solution)/shard_map/transpose | solution.py:440
  (22 shorter events, 0.6 us)
Async XLA Ops:
  0.6 0.7 %copy-start.3 = (s32[8,128]{1,0:T(8,128)S(1)}, s32[8,128]{1,0:T(8,128)}, u32[]{:S(2)}) copy-start(s32[8,128]{1,0:T(8,128)} %param.6) | copy-start | bytes 12292
  2.3 0.9 %copy-start.1 = (bf16[9,48,48]{2,1,0:T(8,128)(2,1)S(1)}, bf16[9,48,48]{2,1,0:T(8,128)(2,1)}, u32[]{:S(2)}) copy-start(bf16[9,48,48]{2,1,0:T(8,128)(2,1)} %param.8) | copy-start | bytes 124420
  4.3 0.9 %copy-start = (bf16[9,48,75]{2,1,0:T(8,128)(2,1)S(1)}, bf16[9,48,75]{2,1,0:T(8,128)(2,1)}, u32[]{:S(2)}) copy-start(bf16[9,48,75]{2,1,0:T(8,128)(2,1)} %param.7) | copy-start | bytes 194404
  7.6 0.9 %copy-start.2 = (bf16[75,8,128]{2,1,0:T(8,128)(2,1)S(1)}, bf16[75,8,128]{2,1,0:T(8,128)(2,1)}, u32[]{:S(2)}) copy-start(bf16[75,8,128]{2,1,0:T(8,128)(2,1)} %param.5) | copy-start | bytes 460804

commit v2 on v1

--- a/solution.py
+++ b/solution.py
@@ -50,38 +50,98 @@
 
 
 def kernel(
-    nlat, nlon, per, owners,
-    f_ref, wa1, wa1n, wa2, tb2, tb2n, tb1, tb1n,
-    out_ref, dx_ref, dw_ref,
-    xm, xg, packs, mine, d1m, d1g, d2m, d2g, hd, dad, am, ae, gbuf, rbuf1, rbuf2, obuf,
-    send_sem, recv_sem, red_send, red_recv,
+    dims, per,
+    x_hbm, m_hbm, w1_hbm, w2_hbm, c_hbm,
+    out_ref, dx_ref, dw1_ref, dw2_ref,
+    x_in, m_in, w1_in, w2_in, c_in, flip, f_ref,
+    wa1, wa1n, wa2, tb2, tb2n, tb1, tb1n,
+    xm, xg, packs, mine, d1m, d1g, d2m, d2g, hd, dad, am, ae,
+    gbuf, rbuf, za, yb, ya, zb, obuf,
+    in_sem, send_sem, recv_sem, red_send, red_recv,
 ):
+    xl_n, z_n, xh_n, y_n, c_n = dims
+    nlat, nlon, group = xl_n * z_n, xh_n * y_n * c_n, xl_n * xh_n * c_n
     lat, lon = lax.axis_index("lat"), lax.axis_index("lon")
+    xl, z = lat // z_n, lat % z_n
+    xh, y, core = lon // (y_n * c_n), (lon // c_n) % y_n, lon % c_n
+    me = (xl * xh_n + xh) * c_n + core
     top, bottom = lat == nlat - 1, lat == 0
     east, west = lax.rem(lon + 1, nlon), lax.rem(lon + nlon - 1, nlon)
+    mirror = nlon - 1 - lon
+    fold_e = lax.rem(2 * nlon - 2 - lon, nlon)
+    fold_w = lax.rem(nlon - lon, nlon)
+
+    def at_z(j):
+        to = lax.rem(z + j, z_n)
+        return xl * z_n + to, lon
+
+    def at_y(j):
+        to = lax.rem(y + j, y_n)
+        return lat, (xh * y_n + to) * c_n + core
+
+    def at_x(j):
+        to = lax.rem(me + j, group)
+        a, b, c = to // (xh_n * c_n), (to // c_n) % xh_n, to % c_n
+        return to, a * z_n + z, (b * y_n + y) * c_n + c
 
     barrier = pltpu.get_barrier_semaphore()
 
     def greet(a, b):
         pl.semaphore_signal(barrier, inc=1, device_id=(a, b), device_id_type=MESH)
 
-    @pl.loop(1, nlon)
-    def _(j):
-        greet(lat, lax.rem(lon + j, nlon))
-
-    @pl.loop(1, nlat)
-    def _(j):
-        greet(lax.rem(lat + j, nlat), lon)
+    for j in range(1, y_n):
+        greet(*at_y(j))
+    for j in range(1, z_n):
+        greet(*at_z(j))
+
+    @pl.when(top)
+    def _():
+        greet(lat, mirror)
+
+        @pl.when(fold_e != lon)
+        def _():
+            greet(lat, fold_e)
+
+        @pl.when(fold_w != lon)
+        def _():
+            greet(lat, fold_w)
+
+    for j in range(1, group):
+        greet(*at_x(j)[1:])
 
     @pl.when(jnp.logical_not(top))
     def _():
+        greet(lat + 1, lon)
         greet(lat + 1, east)
         greet(lat + 1, west)
 
     @pl.when(jnp.logical_not(bottom))
     def _():
+        greet(lat - 1, lon)
         greet(lat - 1, east)
         greet(lat - 1, west)
+
+    greet(lat, east)
+    greet(lat, west)
+
+    loads = [
+        pltpu.make_async_copy(src, dst, in_sem.at[i])
+        for i, (src, dst) in enumerate(
+            ((x_hbm, x_in), (m_hbm, m_in), (c_hbm, c_in), (w1_hbm, w1_in), (w2_hbm, w2_in))
+        )
+    ]
+    for load in loads:
+        load.start()
+
+    for load in loads[:3]:
+        load.wait()
+    sea8 = m_in[...].astype(F32)
+    flip[: CIN * ROWS, :] = x_in[...].astype(F32).reshape(CIN * ROWS, LANES)
+    flip[CIN * ROWS : (CIN + 1) * ROWS, :] = sea8
+    flip[(CIN + 1) * ROWS : KX * ROWS, :] = jnp.zeros(((KX - CIN - 1) * ROWS, LANES), F32)
+    flip[KX * ROWS :, :] = (c_in[...].astype(F32) * sea8[None]).reshape(CH * ROWS, LANES)
+    for r in range(ROWS):
+        f_ref[:, tile(r)] = flip[pl.ds(r, KX + CH, stride=ROWS), :].astype(BF)
 
     cell = lax.broadcasted_iota(jnp.int32, (32, ROWS * LANES), 0)
     place = lax.broadcasted_iota(jnp.int32, (32, ROWS * LANES), 1)
@@ -90,9 +150,10 @@
     mine[0] = picked[:16]
     mine[1] = picked[16:]
 
+    folds = 1 + jnp.where(fold_e != lon, 1, 0) + jnp.where(fold_w != lon, 1, 0)
     pl.semaphore_wait(
         barrier,
-        nlon - 1 + nlat - 1 + jnp.where(top, 0, 2) + jnp.where(bottom, 0, 2),
+        y_n + z_n + group - 3 + 2 + jnp.where(top, folds, 3) + jnp.where(bottom, 0, 3),
     )
 
     def send(src, dst, slot, a, b):
@@ -103,8 +164,6 @@
 
     low, high = f_ref.at[:, tile(0, 2)], f_ref.at[:, tile(ROWS - 2, 2)]
     above, below = xm.at[:, tile(ROWS + 2, 2)], xm.at[:, tile(0, 2)]
-    fold_e = lax.rem(2 * nlon - 2 - lon, nlon)
-    fold_w = lax.rem(nlon - lon, nlon)
 
     @pl.when(jnp.logical_not(top))
     def _():
@@ -112,7 +171,7 @@
 
     @pl.when(top)
     def _():
-        send(high, above, 6, lat, nlon - 1 - lon).start()
+        send(high, above, 6, lat, mirror).start()
 
     @pl.when(jnp.logical_not(bottom))
     def _():
@@ -174,6 +233,40 @@
     lane_to = jnp.where((slot == 3) & top, 1 - j, lane_to)
     good = (slot < 2) | ((slot < 4) & (row_to < EXT)) | ((slot >= 4) & (row_to >= 0))
     goal = jnp.where(good, row_to * LANES + lane_to, -1)
+
+    loads[3].wait()
+    loads[4].wait()
+    gap = jnp.zeros((CH, KX - CIN), F32)
+    k1 = [jnp.concatenate([w1_in[t].astype(F32), gap], axis=1) for t in range(9)]
+    k2 = [w2_in[t].astype(F32) for t in range(9)]
+
+    def square(k, pick):
+        return jnp.concatenate(
+            [jnp.concatenate([k[pick(a, b)] for b in range(3)], axis=1) for a in range(3)], axis=0
+        )
+
+    def plain(a, b):
+        return 3 * a + b
+
+    def turned(a, b):
+        return 8 - 3 * a - b
+
+    def swapped(a, b):
+        return 3 * b + a
+
+    def both(a, b):
+        return 8 - 3 * b - a
+
+    m = square(k1, plain)
+    wa1[...] = m.astype(BF)
+    wa1n[...] = jnp.where(top, square(k1, turned), m).astype(BF)
+    wa2[...] = square(k2, plain).astype(BF)
+    m = square(k2, both)
+    tb2[...] = m.T.astype(BF)
+    tb2n[...] = jnp.where(top, square(k2, swapped), m).T.astype(BF)
+    m = square(k1, both)
+    tb1[...] = m.T.astype(BF)
+    tb1n[...] = jnp.where(top, square(k1, swapped), m).T.astype(BF)
 
     def landed(ref, slot):
         pltpu.make_async_copy(ref, ref, recv_sem.at[slot]).wait()
@@ -269,63 +362,81 @@
     for t in range(TILES):
         a, b = t // 3, t % 3
         gbuf[t // per, (t % per) * 16 : (t % per + 1) * 16, :] = terms[16 * a : 16 * a + 16, tile(b)]
-    if TILES < per * owners:
-        gbuf[owners - 1, (TILES - per * (owners - 1)) * 16 :, :] = jnp.zeros(
-            ((per * owners - TILES) * 16, LANES), BF
-        )
-
-    def reduce_send(src, dst, phase, a, b):
-        return pltpu.make_async_remote_copy(
+    blank = jnp.zeros((16, LANES), BF)
+    for t in range(TILES, per * group):
+        gbuf[t // per, (t % per) * 16 : (t % per + 1) * 16, :] = blank
+
+    def pass_on(src, dst, phase, a, b):
+        pltpu.make_async_remote_copy(
             src_ref=src, dst_ref=dst, send_sem=red_send.at[phase], recv_sem=red_recv.at[phase],
             device_id=(a, b), device_id_type=MESH,
-        )
-
-    @pl.loop(1, nlon)
-    def _(j):
-        peer = lax.rem(lon + j, nlon)
-
-        @pl.when(peer < owners)
-        def _():
-            reduce_send(gbuf.at[peer], rbuf1.at[lon], 0, lat, peer).start()
+        ).start()
+
+    def done(ref, count, sem):
+        some = ref.at[pl.ds(0, count)]
+        pltpu.make_async_copy(some, some, sem).wait()
+
+    def total(ref):
+        return jnp.sum(ref[...].astype(F32), axis=0).astype(BF)
+
+    for j in range(1, group):
+        to, a, b = at_x(j)
+        pass_on(gbuf.at[to], rbuf.at[me], 0, a, b)
+    rbuf[me] = gbuf[me]
 
     sea = f_ref[CIN : CIN + 1, :].astype(F32)
-    out_ref[...] = (gather_rows(nn(wa2[...], hd[...]), ROWS) * sea).astype(BF)
+    res = gather_rows(nn(wa2[...], hd[...]), ROWS) * sea
+    for r in range(ROWS):
+        flip[pl.ds(r, CH, stride=ROWS), :] = res[:, tile(r)]
+    out_ref[...] = flip[: CH * ROWS, :].reshape(CH, ROWS, LANES).astype(BF)
     v = jnp.concatenate(
         [nn(tb1[...], dad[:, tile(0, RIM - 1)]), nn(tb1n[...], dad[:, tile(RIM - 1)])], axis=1
     )
-    dx_ref[...] = gather_rows(v, ROWS).astype(BF)
-
-    owner = lon < owners
-
-    @pl.when(owner)
-    def _():
-        rbuf1[lon] = gbuf[lon]
-        some = rbuf1.at[pl.ds(0, nlon - 1)]
-        pltpu.make_async_copy(some, some, red_recv.at[0]).wait()
-        rbuf2[lat] = jnp.sum(rbuf1[...].astype(F32), axis=0).astype(BF)
-
-        @pl.loop(1, nlat)
-        def _(j):
-            peer = lax.rem(lat + j, nlat)
-            reduce_send(rbuf2.at[lat], rbuf2.at[lat], 1, peer, lon).start()
-
-        some2 = rbuf2.at[pl.ds(0, nlat - 1)]
-        pltpu.make_async_copy(some2, some2, red_recv.at[1]).wait()
-        obuf[lon] = jnp.sum(rbuf2[...].astype(F32), axis=0).astype(BF)
-
-        @pl.loop(1, nlon)
-        def _(j):
-            peer = lax.rem(lon + j, nlon)
-            reduce_send(obuf.at[lon], obuf.at[lon], 2, lat, peer).start()
-
-        got = obuf.at[pl.ds(0, owners - 1)]
-        pltpu.make_async_copy(got, got, red_recv.at[2]).wait()
-
-    @pl.when(jnp.logical_not(owner))
-    def _():
-        pltpu.make_async_copy(obuf, obuf, red_recv.at[2]).wait()
-
-    dw_ref[...] = obuf[...]
+    res = gather_rows(v, ROWS)
+    for r in range(ROWS):
+        flip[pl.ds(r, KX, stride=ROWS), :] = res[:, tile(r)]
+    dx_ref[...] = flip[: CIN * ROWS, :].reshape(CIN, ROWS, LANES).astype(BF)
+
+    half = per * 8
+    done(rbuf, group - 1, red_recv.at[0])
+    part = total(rbuf)
+    za[z] = part[:half]
+    yb[y] = part[half:]
+    for j in range(1, z_n):
+        pass_on(za.at[z], za.at[z], 1, *at_z(j))
+    for j in range(1, y_n):
+        pass_on(yb.at[y], yb.at[y], 2, *at_y(j))
+    done(za, z_n - 1, red_recv.at[1])
+    ya[y] = total(za)
+    for j in range(1, y_n):
+        pass_on(ya.at[y], ya.at[y], 3, *at_y(j))
+    done(yb, y_n - 1, red_recv.at[2])
+    zb[z] = total(yb)
+    for j in range(1, z_n):
+        pass_on(zb.at[z], zb.at[z], 4, *at_z(j))
+    done(ya, y_n - 1, red_recv.at[3])
+    obuf[me, :half] = total(ya)
+    done(zb, z_n - 1, red_recv.at[4])
+    obuf[me, half:] = total(zb)
+    for j in range(1, group):
+        _, a, b = at_x(j)
+        pass_on(obuf.at[me], obuf.at[me], 5, a, b)
+    done(obuf, group - 1, red_recv.at[5])
+
+    factor = 1.0 / math.sqrt(ROWS * LANES * nlat * nlon)
+    for dr in range(3):
+        rows3 = []
+        for a in range(3 * dr, 3 * dr + 3):
+            tiles = range(3 * a, 3 * a + 3)
+            rows3.append(
+                jnp.concatenate(
+                    [obuf[t // per, (t % per) * 16 : (t % per + 1) * 16, :] for t in tiles], axis=1
+                )
+            )
+        grads = jnp.concatenate(rows3, axis=0).astype(F32) * factor
+        for dc in range(3):
+            dw1_ref[3 * dr + dc] = grads[:, dc * KX : dc * KX + CIN]
+            dw2_ref[3 * dr + dc] = grads[:, 3 * KX + dc * CH : 3 * KX + (dc + 1) * CH]
 
     def sent(ref, sem):
         pltpu.make_async_copy(ref, ref, sem).wait()
@@ -357,97 +468,63 @@
         sent(mine.at[0], send_sem.at[2])
         sent(mine.at[1], send_sem.at[3])
 
-    @pl.when(owner)
-    def _():
-        sent(gbuf.at[pl.ds(0, owners - 1)], red_send.at[0])
-        sent(rbuf2.at[pl.ds(0, nlat - 1)], red_send.at[1])
-        sent(rbuf1.at[pl.ds(0, nlon - 1)], red_send.at[2])
-
-    @pl.when(jnp.logical_not(owner))
-    def _():
-        sent(gbuf, red_send.at[0])
-
-
-def stacked(w, pad):
-    w = jnp.pad(w, ((0, 0), (0, 0), (0, 0), (0, pad)))
-    return w.transpose(0, 2, 1, 3).reshape(3 * w.shape[2], 3 * w.shape[3])
-
-
-def body(nlat, nlon, fields, mask, w1, w2, cotangent):
-    sea = mask.astype(BF)[None]
-    field = jnp.concatenate(
-        [fields, sea, jnp.zeros((KX - CIN - 1, ROWS, LANES), BF), cotangent * sea], axis=0
-    ).reshape(KX + CH, ROWS * LANES)
-    top = lax.axis_index("lat") == nlat - 1
-    k1 = w1.reshape(3, 3, CH, CIN)
-    k2 = w2.reshape(3, 3, CH, CH)
-    k1r, k2r = k1[::-1, ::-1], k2[::-1, ::-1]
-    swap = (0, 1, 3, 2)
-    rows = ((0, 0), (0, 0), (0, KX - CIN), (0, 0))
-    wa1 = stacked(k1, KX - CIN)
-    wa1n = stacked(jnp.where(top, k1r, k1), KX - CIN)
-    wa2 = stacked(k2, 0)
-    tb2 = stacked(k2r.transpose(swap), 0)
-    tb2n = stacked(jnp.where(top, k2, k2r).transpose(swap), 0)
-    tb1 = stacked(jnp.pad(k1r.transpose(swap), rows), 0)
-    tb1n = stacked(jnp.pad(jnp.where(top, k1, k1r).transpose(swap), rows), 0)
-
-    per = -(-TILES // nlon)
-    owners = -(-TILES // per)
-    chunk = (per * 16, LANES)
+    done(rbuf, group - 1, red_send.at[0])
+    done(za, z_n - 1, red_send.at[1])
+    done(yb, y_n - 1, red_send.at[2])
+    done(ya, y_n - 1, red_send.at[3])
+    done(zb, z_n - 1, red_send.at[4])
+    done(obuf, group - 1, red_send.at[5])
+
+
+def body(dims, fields, mask, w1, w2, cotangent):
+    xl_n, z_n, xh_n, y_n, c_n = dims
+    group = xl_n * xh_n * c_n
+    per = -(-TILES // (2 * group)) * 2
     wide, slim = EXT * LANES, RIM * LANES
     vm = pl.BlockSpec(memory_space=pltpu.VMEM)
-    out, dx, dw = pl.pallas_call(
-        functools.partial(kernel, nlat, nlon, per, owners),
+    hbm = pl.BlockSpec(memory_space=pl.ANY)
+
+    def held(*shape):
+        return pltpu.VMEM(shape, BF)
+
+    return pl.pallas_call(
+        functools.partial(kernel, dims, per),
         out_shape=(
-            jax.ShapeDtypeStruct((CH, ROWS * LANES), BF),
-            jax.ShapeDtypeStruct((KX, ROWS * LANES), BF),
-            jax.ShapeDtypeStruct((owners,) + chunk, BF),
+            jax.ShapeDtypeStruct((CH, ROWS, LANES), BF),
+            jax.ShapeDtypeStruct((CIN, ROWS, LANES), BF),
+            jax.ShapeDtypeStruct((9, CH, CIN), F32),
+            jax.ShapeDtypeStruct((9, CH, CH), F32),
         ),
-        in_specs=[vm] * 8,
-        out_specs=(vm, vm, vm),
+        in_specs=[hbm] * 5,
+        out_specs=(vm,) * 4,
         scratch_shapes=[
-            pltpu.VMEM((128, wide), BF),
-            pltpu.VMEM((128, wide), BF),
-            pltpu.VMEM((6, 16, 128), BF),
-            pltpu.VMEM((2, 16, 128), BF),
-            pltpu.VMEM((3 * KX, wide), BF),
-            pltpu.VMEM((3 * KX, wide), BF),
-            pltpu.VMEM((3 * CH, wide), BF),
-            pltpu.VMEM((3 * CH, wide), BF),
-            pltpu.VMEM((3 * CH, slim), BF),
-            pltpu.VMEM((3 * CH, slim), BF),
-            pltpu.VMEM((3 * CH, slim), BF),
-            pltpu.VMEM((3 * CH, slim), BF),
-            pltpu.VMEM((owners,) + chunk, BF),
-            pltpu.VMEM((nlon,) + chunk, BF),
-            pltpu.VMEM((nlat,) + chunk, BF),
-            pltpu.VMEM((owners,) + chunk, BF),
-            pltpu.SemaphoreType.DMA((11,)),
-            pltpu.SemaphoreType.DMA((11,)),
-            pltpu.SemaphoreType.DMA((3,)),
-            pltpu.SemaphoreType.DMA((3,)),
+            held(CIN, ROWS, LANES), pltpu.VMEM((ROWS, LANES), jnp.int32),
+            held(9, CH, CIN), held(9, CH, CH), held(CH, ROWS, LANES),
+            pltpu.VMEM(((KX + CH) * ROWS, LANES), F32), held(KX + CH, ROWS * LANES),
+            held(3 * CH, 3 * KX), held(3 * CH, 3 * KX), held(3 * CH, 3 * CH),
+            held(3 * CH, 3 * CH), held(3 * CH, 3 * CH), held(3 * KX, 3 * CH), held(3 * KX, 3 * CH),
+            held(128, wide), held(128, wide), held(6, 16, 128), held(2, 16, 128),
+            held(3 * KX, wide), held(3 * KX, wide), held(3 * CH, wide), held(3 * CH, wide),
+            held(3 * CH, slim), held(3 * CH, slim), held(3 * CH, slim), held(3 * CH, slim),
+            held(group, per * 16, LANES), held(group, per * 16, LANES),
+            held(z_n, per * 8, LANES), held(y_n, per * 8, LANES),
+            held(y_n, per * 8, LANES), held(z_n, per * 8, LANES),
+            held(group, per * 16, LANES),
+            pltpu.SemaphoreType.DMA((5,)),
+            pltpu.SemaphoreType.DMA((11,)), pltpu.SemaphoreType.DMA((11,)),
+            pltpu.SemaphoreType.DMA((6,)), pltpu.SemaphoreType.DMA((6,)),
         ],
         compiler_params=pltpu.CompilerParams(
-            collective_id=0, has_side_effects=True, vmem_limit_bytes=40 * 1024 * 1024
+            collective_id=0, has_side_effects=True, vmem_limit_bytes=56 * 1024 * 1024
         ),
-    )(field, wa1, wa1n, wa2, tb2, tb2n, tb1, tb1n)
-
-    factor = 1.0 / math.sqrt(ROWS * LANES * nlat * nlon)
-    grads = dw.reshape(-1, 16, LANES)[:TILES].reshape(9, 3, 16, LANES).transpose(0, 2, 1, 3)
-    grads = grads.reshape(3 * CH, 3 * LANES).astype(F32) * factor
-    dw1 = grads[:, : 3 * KX].reshape(3, CH, 3, KX)[..., :CIN].transpose(0, 2, 1, 3)
-    dw2 = grads[:, 3 * KX :].reshape(3, CH, 3, CH).transpose(0, 2, 1, 3)
-    return (
-        out.reshape(CH, ROWS, LANES),
-        dx[:CIN].reshape(CIN, ROWS, LANES),
-        dw1.reshape(9, CH, CIN),
-        dw2.reshape(9, CH, CH),
-    )
+    )(fields, mask, w1, w2, cotangent)
 
 
 def solution(mesh):
     in_specs = (P(None, "lat", "lon"), P("lat", "lon"), P(), P(), P(None, "lat", "lon"))
     out_specs = (P(None, "lat", "lon"), P(None, "lat", "lon"), P(), P())
-    run = functools.partial(body, mesh.shape["lat"], mesh.shape["lon"])
+    nlat, nlon = mesh.shape["lat"], mesh.shape["lon"]
+    x_hi = 2 if nlon > 4 else 1
+    dims = (2, nlat // 2, x_hi, nlon // (2 * x_hi), 2)
+    run = functools.partial(body, dims)
     return jax.shard_map(run, mesh=mesh, in_specs=in_specs, out_specs=out_specs, check_vma=False)

time: 55.1 us -> 47.7 us (0.87)
  local copies, waits for them, and re-layouts: 9.98 us -> 3.96 us
  other arithmetic: 1.27 us -> 0 us
    reshape x16 -> x0, local copies, waits for them, and re-layouts: 2.36 us -> none  [the longest x9 1.04 us: stacked(): return w.transpose(0, 2, 1, 3).reshape(3 * w.shape[2], 3 * w.shape[3])]
    transpose x8 -> x0, local copies, waits for them, and re-layouts: 1.91 us -> none  [the longest x2 0.75 us: body(): grads[:, :3 * KX].reshape(3, CH, 3, KX)[..., :CIN].transpose(0, 2, 1, 3)]
    rev x2 -> x0, local copies, waits for them, and re-layouts: 1.64 us -> none  [body(): k1r, k2r = (k1[::-1, ::-1], k2[::-1, ::-1])]
    mul x2 -> x0, other arithmetic: 0.92 us -> none  [the longest x1 0.9 us: body(): cotangent * sea]
    unnamed x15 -> x10, local copies, waits for them, and re-layouts: 3.77 us -> 3.96 us
where the time goes in v2:
time: 47.7 us; the launch traced here: 47.5 us
  Pallas kernels  42.9 us (90%)
  local copies, waits for them, and re-layouts  3.96 us (8%)
  between operations  0.66 us (1%)
    pallas_call x1, Pallas kernels, body(): pl.pallas_call(functools.partial(kernel, dims, per), out_shape=(jax.Shape...  42.9 us
    unnamed x10, local copies, waits for them, and re-layouts  3.96 us

profile of v2, /device:TPU:1, one launch (start us, length us, event | category | flops | bytes accessed | tf_op | source)
XLA Modules:
  0.0 47.5 jit_solution(17023957545021222772)
XLA Ops:
  0.6 42.9 %shard_map.84 = (bf16[48,8,128]{2,1,0:T(8,128)(2,1)}, bf16[75,8,128]{2,1,0:T(8,128)(2,1)}, f32[9,48,75]{2,1,0:T(8,128)}, f32[9,48,48]{2,1,0:T(8,128)}) custom-call(bf16[75,8,128]{2,1,0:T(8,128)(2,1)} %x_hbm.1, s32[8,128]{1,0:T(8,128)} %m_hbm.1, bf16[9,48,75]{2,1,0:T(8,128)(2,1)} %w1_hbm.1, bf16[9,48,48]{2,1,0:T(8,128)(2,1)} %w2_hbm.1, bf16[48,8,128]{2,1,0:T(8,128)(2,1)} %c_hbm.1), custom_call_target="tpu_custom_call" | custom-call | tf_op jit(solution)/shard_map/pallas_call | solution.py:490
  43.5 0.0 copy-start.2
  43.5 0.0 copy-start.1
  43.5 1.6 %copy.13 = bf16[48,8,128]{2,1,0:T(8,128)(2,1)} copy(bf16[48,8,128]{2,1,0:T(8,128)(2,1)} %get-tuple-element.8) | data formatting | bytes 196608
  45.1 0.0 copy-done.2
  45.1 0.7 %copy.14 = bf16[75,8,128]{2,1,0:T(8,128)(2,1)} copy(bf16[75,8,128]{2,1,0:T(8,128)(2,1)S(1)} %copy-done.2) | data formatting | bytes 307200
  45.8 0.0 copy-done.1
  45.8 0.0 copy-start
  45.8 0.7 %copy.15 = f32[9,48,75]{2,1,0:T(8,128)} copy(f32[9,48,75]{2,1,0:T(8,128)S(1)} %copy-done.1) | data formatting | bytes 259200
  46.5 0.3 copy-done
  46.8 0.7 %copy.16 = f32[9,48,48]{2,1,0:T(8,128)} copy(f32[9,48,48]{2,1,0:T(8,128)S(1)} %copy-done) | data formatting | bytes 165888
Async XLA Ops:
  43.5 1.6 %copy-start.2 = (bf16[75,8,128]{2,1,0:T(8,128)(2,1)S(1)}, bf16[75,8,128]{2,1,0:T(8,128)(2,1)}, u32[]{:S(2)}) copy-start(bf16[75,8,128]{2,1,0:T(8,128)(2,1)} %get-tuple-element.9) | copy-start | bytes 460804
  43.5 2.3 %copy-start.1 = (f32[9,48,75]{2,1,0:T(8,128)S(1)}, f32[9,48,75]{2,1,0:T(8,128)}, u32[]{:S(2)}) copy-start(f32[9,48,75]{2,1,0:T(8,128)} %get-tuple-element.10) | copy-start | bytes 388804
  45.8 1.0 %copy-start = (f32[9,48,48]{2,1,0:T(8,128)S(1)}, f32[9,48,48]{2,1,0:T(8,128)}, u32[]{:S(2)}) copy-start(f32[9,48,48]{2,1,0:T(8,128)} %get-tuple-element.11) | copy-start | bytes 248836

commit v3 on v2

--- a/solution.py
+++ b/solution.py
@@ -49,16 +49,21 @@
     return y[:c, :n] + y[c : 2 * c, LANES : LANES + n] + y[2 * c :, 2 * LANES : 2 * LANES + n]
 
 
+def far_first(n):
+    return sorted(range(1, n), key=lambda j: -min(j, n - j))
+
+
 def kernel(
-    dims, per,
+    dims,
     x_hbm, m_hbm, w1_hbm, w2_hbm, c_hbm,
-    out_ref, dx_ref, dw1_ref, dw2_ref,
+    out_ref, dx_ref, dw_ref,
     x_in, m_in, w1_in, w2_in, c_in, flip, f_ref,
     wa1, wa1n, wa2, tb2, tb2n, tb1, tb1n,
     xm, xg, packs, mine, d1m, d1g, d2m, d2g, hd, dad, am, ae,
-    gbuf, rbuf, za, yb, ya, zb, obuf,
-    in_sem, send_sem, recv_sem, red_send, red_recv,
+    gbuf, rbuf, ex1, ex2, obuf,
+    in_sem, out_sem, send_sem, recv_sem, *red,
 ):
+    sem_rs, sem_x1, sem_x2, sem_ag = red[0:2], red[2:4], red[4:6], red[6:8]
     xl_n, z_n, xh_n, y_n, c_n = dims
     nlat, nlon, group = xl_n * z_n, xh_n * y_n * c_n, xl_n * xh_n * c_n
     lat, lon = lax.axis_index("lat"), lax.axis_index("lon")
@@ -84,46 +89,6 @@
         a, b, c = to // (xh_n * c_n), (to // c_n) % xh_n, to % c_n
         return to, a * z_n + z, (b * y_n + y) * c_n + c
 
-    barrier = pltpu.get_barrier_semaphore()
-
-    def greet(a, b):
-        pl.semaphore_signal(barrier, inc=1, device_id=(a, b), device_id_type=MESH)
-
-    for j in range(1, y_n):
-        greet(*at_y(j))
-    for j in range(1, z_n):
-        greet(*at_z(j))
-
-    @pl.when(top)
-    def _():
-        greet(lat, mirror)
-
-        @pl.when(fold_e != lon)
-        def _():
-            greet(lat, fold_e)
-
-        @pl.when(fold_w != lon)
-        def _():
-            greet(lat, fold_w)
-
-    for j in range(1, group):
-        greet(*at_x(j)[1:])
-
-    @pl.when(jnp.logical_not(top))
-    def _():
-        greet(lat + 1, lon)
-        greet(lat + 1, east)
-        greet(lat + 1, west)
-
-    @pl.when(jnp.logical_not(bottom))
-    def _():
-        greet(lat - 1, lon)
-        greet(lat - 1, east)
-        greet(lat - 1, west)
-
-    greet(lat, east)
-    greet(lat, west)
-
     loads = [
         pltpu.make_async_copy(src, dst, in_sem.at[i])
         for i, (src, dst) in enumerate(
@@ -132,6 +97,45 @@
     ]
     for load in loads:
         load.start()
+
+    barrier = pltpu.get_barrier_semaphore()
+
+    def greet(a, b):
+        pl.semaphore_signal(barrier, inc=1, device_id=(a, b), device_id_type=MESH)
+
+    @pl.when(top)
+    def _():
+        greet(lat, mirror)
+
+        @pl.when(fold_e != lon)
+        def _():
+            greet(lat, fold_e)
+
+        @pl.when(fold_w != lon)
+        def _():
+            greet(lat, fold_w)
+
+    for j in far_first(y_n):
+        greet(*at_y(j))
+    for j in far_first(z_n):
+        greet(*at_z(j))
+    for j in range(1, group):
+        greet(*at_x(j)[1:])
+
+    @pl.when(jnp.logical_not(top))
+    def _():
+        greet(lat + 1, east)
+        greet(lat + 1, west)
+        greet(lat + 1, lon)
+
+    @pl.when(jnp.logical_not(bottom))
+    def _():
+        greet(lat - 1, east)
+        greet(lat - 1, west)
+        greet(lat - 1, lon)
+
+    greet(lat, east)
+    greet(lat, west)
 
     for load in loads[:3]:
         load.wait()
@@ -165,48 +169,46 @@
     low, high = f_ref.at[:, tile(0, 2)], f_ref.at[:, tile(ROWS - 2, 2)]
     above, below = xm.at[:, tile(ROWS + 2, 2)], xm.at[:, tile(0, 2)]
 
+    @pl.when(top)
+    def _():
+        @pl.when(fold_e != lon)
+        def _():
+            send(mine.at[0], packs.at[3], 9, lat, fold_e).start()
+
+        @pl.when(fold_w != lon)
+        def _():
+            send(mine.at[1], packs.at[2], 10, lat, fold_w).start()
+
+        send(high, above, 6, lat, mirror).start()
+
+        @pl.when(fold_e == lon)
+        def _():
+            packs[3] = mine[0]
+
+        @pl.when(fold_w == lon)
+        def _():
+            packs[2] = mine[1]
+
+    @pl.when(jnp.logical_not(bottom))
+    def _():
+        send(mine.at[0], packs.at[2], 2, lat - 1, east).start()
+        send(mine.at[1], packs.at[3], 3, lat - 1, west).start()
+
     @pl.when(jnp.logical_not(top))
     def _():
-        send(high, below, 7, lat + 1, lon).start()
-
-    @pl.when(top)
-    def _():
-        send(high, above, 6, lat, mirror).start()
-
-    @pl.when(jnp.logical_not(bottom))
-    def _():
-        send(low, above, 8, lat - 1, lon).start()
+        send(mine.at[0], packs.at[4], 4, lat + 1, east).start()
+        send(mine.at[1], packs.at[5], 5, lat + 1, west).start()
 
     send(mine.at[0], packs.at[0], 0, lat, east).start()
     send(mine.at[1], packs.at[1], 1, lat, west).start()
 
+    @pl.when(jnp.logical_not(top))
+    def _():
+        send(high, below, 7, lat + 1, lon).start()
+
     @pl.when(jnp.logical_not(bottom))
     def _():
-        send(mine.at[0], packs.at[2], 2, lat - 1, east).start()
-        send(mine.at[1], packs.at[3], 3, lat - 1, west).start()
-
-    @pl.when(jnp.logical_not(top))
-    def _():
-        send(mine.at[0], packs.at[4], 4, lat + 1, east).start()
-        send(mine.at[1], packs.at[5], 5, lat + 1, west).start()
-
-    @pl.when(top)
-    def _():
-        @pl.when(fold_e != lon)
-        def _():
-            send(mine.at[0], packs.at[3], 9, lat, fold_e).start()
-
-        @pl.when(fold_w != lon)
-        def _():
-            send(mine.at[1], packs.at[2], 10, lat, fold_w).start()
-
-        @pl.when(fold_e == lon)
-        def _():
-            packs[3] = mine[0]
-
-        @pl.when(fold_w == lon)
-        def _():
-            packs[2] = mine[1]
+        send(low, above, 8, lat - 1, lon).start()
 
     @pl.when(bottom)
     def _():
@@ -361,14 +363,11 @@
     terms = jnp.concatenate([term1, term2], axis=1).astype(BF)
     for t in range(TILES):
         a, b = t // 3, t % 3
-        gbuf[t // per, (t % per) * 16 : (t % per + 1) * 16, :] = terms[16 * a : 16 * a + 16, tile(b)]
-    blank = jnp.zeros((16, LANES), BF)
-    for t in range(TILES, per * group):
-        gbuf[t // per, (t % per) * 16 : (t % per + 1) * 16, :] = blank
-
-    def pass_on(src, dst, phase, a, b):
+        gbuf[t // group, t % group] = terms[16 * a : 16 * a + 16, tile(b)]
+
+    def pass_on(src, dst, sems, p, a, b):
         pltpu.make_async_remote_copy(
-            src_ref=src, dst_ref=dst, send_sem=red_send.at[phase], recv_sem=red_recv.at[phase],
+            src_ref=src, dst_ref=dst, send_sem=sems[0].at[p], recv_sem=sems[1].at[p],
             device_id=(a, b), device_id_type=MESH,
         ).start()
 
@@ -376,67 +375,84 @@
         some = ref.at[pl.ds(0, count)]
         pltpu.make_async_copy(some, some, sem).wait()
 
-    def total(ref):
-        return jnp.sum(ref[...].astype(F32), axis=0).astype(BF)
-
-    for j in range(1, group):
-        to, a, b = at_x(j)
-        pass_on(gbuf.at[to], rbuf.at[me], 0, a, b)
-    rbuf[me] = gbuf[me]
+    def total(ref, p, count):
+        acc = ref[p, 0].astype(F32)
+        for i in range(1, count):
+            acc = acc + ref[p, i].astype(F32)
+        return acc.astype(BF)
+
+    def only(test, always, f):
+        if always:
+            f()
+        else:
+            pl.when(test)(f)
+
+    parts = -(-TILES // group)
+    count = [min(group, TILES - p * group) for p in range(parts)]
+    first = [(z_n, z, at_z) if p % 2 == 0 else (y_n, y, at_y) for p in range(parts)]
+    second = [(y_n, y, at_y) if p % 2 == 0 else (z_n, z, at_z) for p in range(parts)]
+
+    for p in range(parts):
+        for j in range(1, group):
+            to, a, b = at_x(j)
+            only(
+                to < count[p], count[p] == group,
+                functools.partial(pass_on, gbuf.at[p, to], rbuf.at[p, me], sem_rs, p, a, b),
+            )
 
     sea = f_ref[CIN : CIN + 1, :].astype(F32)
     res = gather_rows(nn(wa2[...], hd[...]), ROWS) * sea
     for r in range(ROWS):
         flip[pl.ds(r, CH, stride=ROWS), :] = res[:, tile(r)]
-    out_ref[...] = flip[: CH * ROWS, :].reshape(CH, ROWS, LANES).astype(BF)
+    c_in[...] = flip[: CH * ROWS, :].reshape(CH, ROWS, LANES).astype(BF)
+    stores = [pltpu.make_async_copy(c_in, out_ref, in_sem.at[0])]
+    stores[0].start()
     v = jnp.concatenate(
         [nn(tb1[...], dad[:, tile(0, RIM - 1)]), nn(tb1n[...], dad[:, tile(RIM - 1)])], axis=1
     )
     res = gather_rows(v, ROWS)
     for r in range(ROWS):
         flip[pl.ds(r, KX, stride=ROWS), :] = res[:, tile(r)]
-    dx_ref[...] = flip[: CIN * ROWS, :].reshape(CIN, ROWS, LANES).astype(BF)
-
-    half = per * 8
-    done(rbuf, group - 1, red_recv.at[0])
-    part = total(rbuf)
-    za[z] = part[:half]
-    yb[y] = part[half:]
-    for j in range(1, z_n):
-        pass_on(za.at[z], za.at[z], 1, *at_z(j))
-    for j in range(1, y_n):
-        pass_on(yb.at[y], yb.at[y], 2, *at_y(j))
-    done(za, z_n - 1, red_recv.at[1])
-    ya[y] = total(za)
-    for j in range(1, y_n):
-        pass_on(ya.at[y], ya.at[y], 3, *at_y(j))
-    done(yb, y_n - 1, red_recv.at[2])
-    zb[z] = total(yb)
-    for j in range(1, z_n):
-        pass_on(zb.at[z], zb.at[z], 4, *at_z(j))
-    done(ya, y_n - 1, red_recv.at[3])
-    obuf[me, :half] = total(ya)
-    done(zb, z_n - 1, red_recv.at[4])
-    obuf[me, half:] = total(zb)
-    for j in range(1, group):
-        _, a, b = at_x(j)
-        pass_on(obuf.at[me], obuf.at[me], 5, a, b)
-    done(obuf, group - 1, red_recv.at[5])
-
-    factor = 1.0 / math.sqrt(ROWS * LANES * nlat * nlon)
-    for dr in range(3):
-        rows3 = []
-        for a in range(3 * dr, 3 * dr + 3):
-            tiles = range(3 * a, 3 * a + 3)
-            rows3.append(
-                jnp.concatenate(
-                    [obuf[t // per, (t % per) * 16 : (t % per + 1) * 16, :] for t in tiles], axis=1
-                )
+    x_in[...] = flip[: CIN * ROWS, :].reshape(CIN, ROWS, LANES).astype(BF)
+    stores.append(pltpu.make_async_copy(x_in, dx_ref, in_sem.at[1]))
+    stores[1].start()
+
+    def hop(p, source, arrived, sem, held_as, axis, sems):
+        length, at, peer = axis
+
+        def go():
+            done(source.at[p], arrived - 1, sem.at[p])
+            held_as[p, at] = total(source, p, arrived)
+            for j in far_first(length):
+                pass_on(held_as.at[p, at], held_as.at[p, at], sems, p, *peer(j))
+
+        only(me < count[p], count[p] == group, go)
+
+    for p in range(parts):
+        def own(p=p):
+            rbuf[p, me] = gbuf[p, me]
+
+        only(me < count[p], count[p] == group, own)
+        hop(p, rbuf, group, sem_rs[1], ex1, first[p], sem_x1)
+    for p in range(parts):
+        hop(p, ex1, first[p][0], sem_x1[1], ex2, second[p], sem_x2)
+    everyone = (group, me, lambda j: at_x(j)[1:])
+    for p in range(parts):
+        hop(p, ex2, second[p][0], sem_x2[1], obuf, everyone, sem_ag)
+    for p in range(parts):
+        if count[p] == group:
+            done(obuf.at[p], group - 1, sem_ag[1].at[p])
+        else:
+            pl.when(me < count[p])(
+                functools.partial(done, obuf.at[p], count[p] - 1, sem_ag[1].at[p])
             )
-        grads = jnp.concatenate(rows3, axis=0).astype(F32) * factor
-        for dc in range(3):
-            dw1_ref[3 * dr + dc] = grads[:, dc * KX : dc * KX + CIN]
-            dw2_ref[3 * dr + dc] = grads[:, 3 * KX + dc * CH : 3 * KX + (dc + 1) * CH]
+            pl.when(me >= count[p])(
+                functools.partial(done, obuf.at[p], count[p], sem_ag[1].at[p])
+            )
+        n = count[p]
+        move = pltpu.make_async_copy(obuf.at[p, pl.ds(0, n)], dw_ref.at[p, pl.ds(0, n)], out_sem.at[p])
+        move.start()
+        stores.append(move)
 
     def sent(ref, sem):
         pltpu.make_async_copy(ref, ref, sem).wait()
@@ -468,35 +484,77 @@
         sent(mine.at[0], send_sem.at[2])
         sent(mine.at[1], send_sem.at[3])
 
-    done(rbuf, group - 1, red_send.at[0])
-    done(za, z_n - 1, red_send.at[1])
-    done(yb, y_n - 1, red_send.at[2])
-    done(ya, y_n - 1, red_send.at[3])
-    done(zb, z_n - 1, red_send.at[4])
-    done(obuf, group - 1, red_send.at[5])
+    for p in range(parts):
+        n = count[p]
+        if n == group:
+            done(gbuf.at[p], group - 1, sem_rs[0].at[p])
+        else:
+            pl.when(me < n)(functools.partial(done, gbuf.at[p], n - 1, sem_rs[0].at[p]))
+            pl.when(me >= n)(functools.partial(done, gbuf.at[p], n, sem_rs[0].at[p]))
+
+        def drain(p=p):
+            done(ex1.at[p], first[p][0] - 1, sem_x1[0].at[p])
+            done(ex2.at[p], second[p][0] - 1, sem_x2[0].at[p])
+            done(rbuf.at[p], group - 1, sem_ag[0].at[p])
+
+        only(me < n, n == group, drain)
+    for store in stores:
+        store.wait()
+
+
+def finish(
+    factor, parts, group,
+    out_hbm, dx_hbm, dw_hbm, out_ref, dx_ref, dw1_ref, dw2_ref, tiles, dw1, dw2, sem
+):
+    get = pltpu.make_async_copy(dw_hbm, tiles, sem.at[0])
+    get.start()
+    moves = [
+        pltpu.make_async_copy(src, dst, sem.at[i])
+        for i, (src, dst) in enumerate(
+            ((out_hbm, out_ref), (dx_hbm, dx_ref), (dw1, dw1_ref), (dw2, dw2_ref)), 1
+        )
+    ]
+    moves[0].start()
+    moves[1].start()
+    get.wait()
+    for dr in range(3):
+        grads = jnp.concatenate(
+            [
+                jnp.concatenate(
+                    [tiles[t // group, t % group] for t in range(3 * a, 3 * a + 3)], axis=1
+                )
+                for a in range(3 * dr, 3 * dr + 3)
+            ],
+            axis=0,
+        ).astype(F32) * factor
+        for dc in range(3):
+            dw1[3 * dr + dc] = grads[:, dc * KX : dc * KX + CIN]
+            dw2[3 * dr + dc] = grads[:, 3 * KX + dc * CH : 3 * KX + (dc + 1) * CH]
+    moves[2].start()
+    moves[3].start()
+    for move in moves:
+        move.wait()
 
 
 def body(dims, fields, mask, w1, w2, cotangent):
     xl_n, z_n, xh_n, y_n, c_n = dims
     group = xl_n * xh_n * c_n
-    per = -(-TILES // (2 * group)) * 2
-    wide, slim = EXT * LANES, RIM * LANES
-    vm = pl.BlockSpec(memory_space=pltpu.VMEM)
+    parts = -(-TILES // group)
+    wide, slim, ring = EXT * LANES, RIM * LANES, max(y_n, z_n)
     hbm = pl.BlockSpec(memory_space=pl.ANY)
 
     def held(*shape):
         return pltpu.VMEM(shape, BF)
 
-    return pl.pallas_call(
-        functools.partial(kernel, dims, per),
-        out_shape=(
-            jax.ShapeDtypeStruct((CH, ROWS, LANES), BF),
-            jax.ShapeDtypeStruct((CIN, ROWS, LANES), BF),
-            jax.ShapeDtypeStruct((9, CH, CIN), F32),
-            jax.ShapeDtypeStruct((9, CH, CH), F32),
-        ),
+    fields_like = (
+        jax.ShapeDtypeStruct((CH, ROWS, LANES), BF),
+        jax.ShapeDtypeStruct((CIN, ROWS, LANES), BF),
+    )
+    out, dx, dw = pl.pallas_call(
+        functools.partial(kernel, dims),
+        out_shape=fields_like + (jax.ShapeDtypeStruct((parts, group, 16, LANES), BF),),
         in_specs=[hbm] * 5,
-        out_specs=(vm,) * 4,
+        out_specs=(hbm,) * 3,
         scratch_shapes=[
             held(CIN, ROWS, LANES), pltpu.VMEM((ROWS, LANES), jnp.int32),
             held(9, CH, CIN), held(9, CH, CH), held(CH, ROWS, LANES),
@@ -506,18 +564,32 @@
             held(128, wide), held(128, wide), held(6, 16, 128), held(2, 16, 128),
             held(3 * KX, wide), held(3 * KX, wide), held(3 * CH, wide), held(3 * CH, wide),
             held(3 * CH, slim), held(3 * CH, slim), held(3 * CH, slim), held(3 * CH, slim),
-            held(group, per * 16, LANES), held(group, per * 16, LANES),
-            held(z_n, per * 8, LANES), held(y_n, per * 8, LANES),
-            held(y_n, per * 8, LANES), held(z_n, per * 8, LANES),
-            held(group, per * 16, LANES),
-            pltpu.SemaphoreType.DMA((5,)),
+            held(parts, group, 16, LANES), held(parts, group, 16, LANES),
+            held(parts, ring, 16, LANES), held(parts, ring, 16, LANES),
+            held(parts, group, 16, LANES),
+            pltpu.SemaphoreType.DMA((5,)), pltpu.SemaphoreType.DMA((parts,)),
             pltpu.SemaphoreType.DMA((11,)), pltpu.SemaphoreType.DMA((11,)),
-            pltpu.SemaphoreType.DMA((6,)), pltpu.SemaphoreType.DMA((6,)),
-        ],
+        ] + [pltpu.SemaphoreType.DMA((parts,))] * 8,
         compiler_params=pltpu.CompilerParams(
             collective_id=0, has_side_effects=True, vmem_limit_bytes=56 * 1024 * 1024
         ),
     )(fields, mask, w1, w2, cotangent)
+    factor = 1.0 / math.sqrt(ROWS * LANES * xl_n * z_n * xh_n * y_n * c_n)
+    return pl.pallas_call(
+        functools.partial(finish, factor, parts, group),
+        out_shape=fields_like + (
+            jax.ShapeDtypeStruct((9, CH, CIN), F32),
+            jax.ShapeDtypeStruct((9, CH, CH), F32),
+        ),
+        in_specs=[hbm] * 3,
+        out_specs=(hbm,) * 4,
+        scratch_shapes=[
+            held(parts, group, 16, LANES),
+            pltpu.VMEM((9, CH, CIN), F32), pltpu.VMEM((9, CH, CH), F32),
+            pltpu.SemaphoreType.DMA((5,)),
+        ],
+        compiler_params=pltpu.CompilerParams(vmem_limit_bytes=56 * 1024 * 1024),
+    )(out, dx, dw)
 
 
 def solution(mesh):

time: 47.7 us -> 49.7 us (1.042)
  Pallas kernels: 42.9 us -> 48.9 us
  local copies, waits for them, and re-layouts: 3.96 us -> 0 us
    pallas_call x1 -> x2, Pallas kernels: 42.9 us -> 48.9 us  [the longest x1 40.1 us: body(): pl.pallas_call(functools.partial(kernel, dims), out_shape=fields_like + (...]
    unnamed x10 -> x0, local copies, waits for them, and re-layouts: 3.96 us -> none
where the time goes in v3:
time: 49.7 us; the launch traced here: 49.6 us
  Pallas kernels  48.9 us (98%)
  between operations  0.64 us (1%)
    pallas_call x1, Pallas kernels, body(): pl.pallas_call(functools.partial(kernel, dims), out_shape=fields_like + (...  40.1 us
    pallas_call x1, Pallas kernels, body(): pl.pallas_call(functools.partial(finish, factor, parts, group), out_shape...  8.78 us

profile of v3, /device:TPU:1, one launch (start us, length us, event | category | flops | bytes accessed | tf_op | source)
XLA Modules:
  0.0 49.6 jit_solution(8179158324422632986)
XLA Ops:
  0.6 40.1 %shard_map.84 = (bf16[48,8,128]{2,1,0:T(8,128)(2,1)}, bf16[75,8,128]{2,1,0:T(8,128)(2,1)}, bf16[4,8,16,128]{3,2,1,0:T(8,128)(2,1)}) custom-call(bf16[75,8,128]{2,1,0:T(8,128)(2,1)} %x_hbm.1, s32[8,128]{1,0:T(8,128)} %m_hbm.1, bf16[9,48,75]{2,1,0:T(8,128)(2,1)} %w1_hbm.1, bf16[9,48,48]{2,1,0:T(8,128)(2,1)} %w2_hbm.1, bf16[48,8,128]{2,1,0:T(8,128)(2,1)} %c_hbm.1), custom_call_target="tpu_custom_call" | custom-call | tf_op jit(solution)/shard_map/pallas_call | solution.py:553
  40.8 8.8 %shard_map.85 = (bf16[48,8,128]{2,1,0:T(8,128)(2,1)}, bf16[75,8,128]{2,1,0:T(8,128)(2,1)}, f32[9,48,75]{2,1,0:T(8,128)}, f32[9,48,48]{2,1,0:T(8,128)}) custom-call(bf16[48,8,128]{2,1,0:T(8,128)(2,1)} %get-tuple-element.7.out_hbm, bf16[75,8,128]{2,1,0:T(8,128)(2,1)} %get-tuple-element.8.dx_hbm, bf16[4,8,16,128]{3,2,1,0:T(8,128)(2,1)} %get-tuple-element.9.dw_hbm), custom_call_target="tpu_custom_call" | custom-call | tf_op jit(solution)/shard_map/pallas_call | solution.py:578

commit v4 on v3

--- a/solution.py
+++ b/solution.py
@@ -504,18 +504,19 @@
 
 def finish(
     factor, parts, group,
-    out_hbm, dx_hbm, dw_hbm, out_ref, dx_ref, dw1_ref, dw2_ref, tiles, dw1, dw2, sem
+    out_in, dx_in, dw_in, out_ref, dx_ref, dw1_ref, dw2_ref,
+    tiles, dw1, dw2, get_sem, put_sem,
 ):
-    get = pltpu.make_async_copy(dw_hbm, tiles, sem.at[0])
-    get.start()
-    moves = [
-        pltpu.make_async_copy(src, dst, sem.at[i])
+    get = pltpu.make_async_copy(dw_in, tiles, get_sem)
+    puts = [
+        pltpu.make_async_copy(src, dst, put_sem.at[i])
         for i, (src, dst) in enumerate(
-            ((out_hbm, out_ref), (dx_hbm, dx_ref), (dw1, dw1_ref), (dw2, dw2_ref)), 1
+            ((dw1, dw1_ref), (dw2, dw2_ref), (out_in, out_ref), (dx_in, dx_ref))
         )
     ]
-    moves[0].start()
-    moves[1].start()
+    get.start()
+    puts[2].start()
+    puts[3].start()
     get.wait()
     for dr in range(3):
         grads = jnp.concatenate(
@@ -530,18 +531,19 @@
         for dc in range(3):
             dw1[3 * dr + dc] = grads[:, dc * KX : dc * KX + CIN]
             dw2[3 * dr + dc] = grads[:, 3 * KX + dc * CH : 3 * KX + (dc + 1) * CH]
-    moves[2].start()
-    moves[3].start()
-    for move in moves:
-        move.wait()
-
-
-def body(dims, fields, mask, w1, w2, cotangent):
+    puts[0].start()
+    puts[1].start()
+    for put in puts:
+        put.wait()
+
+
+def body(dims, *inputs):
     xl_n, z_n, xh_n, y_n, c_n = dims
     group = xl_n * xh_n * c_n
     parts = -(-TILES // group)
     wide, slim, ring = EXT * LANES, RIM * LANES, max(y_n, z_n)
-    hbm = pl.BlockSpec(memory_space=pl.ANY)
+    anywhere = pl.BlockSpec(memory_space=pl.ANY)
+    hbm = pl.BlockSpec(memory_space=pltpu.HBM)
 
     def held(*shape):
         return pltpu.VMEM(shape, BF)
@@ -554,7 +556,7 @@
         functools.partial(kernel, dims),
         out_shape=fields_like + (jax.ShapeDtypeStruct((parts, group, 16, LANES), BF),),
         in_specs=[hbm] * 5,
-        out_specs=(hbm,) * 3,
+        out_specs=(anywhere,) * 3,
         scratch_shapes=[
             held(CIN, ROWS, LANES), pltpu.VMEM((ROWS, LANES), jnp.int32),
             held(9, CH, CIN), held(9, CH, CH), held(CH, ROWS, LANES),
@@ -571,9 +573,9 @@
             pltpu.SemaphoreType.DMA((11,)), pltpu.SemaphoreType.DMA((11,)),
         ] + [pltpu.SemaphoreType.DMA((parts,))] * 8,
         compiler_params=pltpu.CompilerParams(
-            collective_id=0, has_side_effects=True, vmem_limit_bytes=56 * 1024 * 1024
+            collective_id=0, has_side_effects=True, vmem_limit_bytes=24 * 1024 * 1024
         ),
-    )(fields, mask, w1, w2, cotangent)
+    )(*(pltpu.with_memory_space_constraint(v, pltpu.HBM) for v in inputs))
     factor = 1.0 / math.sqrt(ROWS * LANES * xl_n * z_n * xh_n * y_n * c_n)
     return pl.pallas_call(
         functools.partial(finish, factor, parts, group),
@@ -581,14 +583,14 @@
             jax.ShapeDtypeStruct((9, CH, CIN), F32),
             jax.ShapeDtypeStruct((9, CH, CH), F32),
         ),
-        in_specs=[hbm] * 3,
+        in_specs=[anywhere] * 3,
         out_specs=(hbm,) * 4,
         scratch_shapes=[
             held(parts, group, 16, LANES),
             pltpu.VMEM((9, CH, CIN), F32), pltpu.VMEM((9, CH, CH), F32),
-            pltpu.SemaphoreType.DMA((5,)),
+            pltpu.SemaphoreType.DMA, pltpu.SemaphoreType.DMA((4,)),
         ],
-        compiler_params=pltpu.CompilerParams(vmem_limit_bytes=56 * 1024 * 1024),
+        compiler_params=pltpu.CompilerParams(vmem_limit_bytes=8 * 1024 * 1024),
     )(out, dx, dw)
 
 

time: 49.7 us -> 41.5 us (0.84)
  Pallas kernels: 48.9 us -> 40.8 us
    pallas_call x1, Pallas kernels: 8.78 us -> 1.17 us  [body(): pl.pallas_call(functools.partial(finish, factor, parts, group), out_shape...]
    pallas_call x1, Pallas kernels: 40.1 us -> 39.6 us  [body(): pl.pallas_call(functools.partial(kernel, dims), out_shape=fields_like + (...]
where the time goes in v4:
time: 41.5 us; the launch traced here: 41.4 us
  Pallas kernels  40.8 us (98%)
  between operations  0.64 us (2%)
    pallas_call x1, Pallas kernels, body(): pl.pallas_call(functools.partial(kernel, dims), out_shape=fields_like + (...  39.6 us
    pallas_call x1, Pallas kernels, body(): pl.pallas_call(functools.partial(finish, factor, parts, group), out_shape...  1.17 us

profile of v4, /device:TPU:1, one launch (start us, length us, event | category | flops | bytes accessed | tf_op | source)
XLA Modules:
  0.0 41.4 jit_solution(12521429463782843682)
XLA Ops:
  0.6 39.6 %shard_map.84 = (bf16[48,8,128]{2,1,0:T(8,128)(2,1)S(1)}, bf16[75,8,128]{2,1,0:T(8,128)(2,1)S(1)}, bf16[4,8,16,128]{3,2,1,0:T(8,128)(2,1)S(1)}) custom-call(bf16[75,8,128]{2,1,0:T(8,128)(2,1)} %x_hbm.1, s32[8,128]{1,0:T(8,128)} %m_hbm.1, bf16[9,48,75]{2,1,0:T(8,128)(2,1)} %w1_hbm.1, bf16[9,48,48]{2,1,0:T(8,128)(2,1)} %w2_hbm.1, bf16[48,8,128]{2,1,0:T(8,128)(2,1)} %c_hbm.1), custom_call_target="tpu_custom_call" | custom-call | tf_op jit(solution)/shard_map/pallas_call | solution.py:555
  40.2 1.2 %shard_map.85 = (bf16[48,8,128]{2,1,0:T(8,128)(2,1)}, bf16[75,8,128]{2,1,0:T(8,128)(2,1)}, f32[9,48,75]{2,1,0:T(8,128)}, f32[9,48,48]{2,1,0:T(8,128)}) custom-call(bf16[48,8,128]{2,1,0:T(8,128)(2,1)S(1)} %get-tuple-element.7.out_in, bf16[75,8,128]{2,1,0:T(8,128)(2,1)S(1)} %get-tuple-element.8.dx_in, bf16[4,8,16,128]{3,2,1,0:T(8,128)(2,1)S(1)} %get-tuple-element.9.dw_in), custom_call_target="tpu_custom_call" | custom-call | tf_op jit(solution)/shard_map/pallas_call | solution.py:580

commit v5 on v4

--- a/solution.py
+++ b/solution.py
@@ -179,8 +179,6 @@
         def _():
             send(mine.at[1], packs.at[2], 10, lat, fold_w).start()
 
-        send(high, above, 6, lat, mirror).start()
-
         @pl.when(fold_e == lon)
         def _():
             packs[3] = mine[0]
@@ -209,6 +207,10 @@
     @pl.when(jnp.logical_not(bottom))
     def _():
         send(low, above, 8, lat - 1, lon).start()
+
+    @pl.when(top)
+    def _():
+        send(high, above, 6, lat, mirror).start()
 
     @pl.when(bottom)
     def _():
@@ -389,17 +391,38 @@
 
     parts = -(-TILES // group)
     count = [min(group, TILES - p * group) for p in range(parts)]
-    first = [(z_n, z, at_z) if p % 2 == 0 else (y_n, y, at_y) for p in range(parts)]
-    second = [(y_n, y, at_y) if p % 2 == 0 else (z_n, z, at_z) for p in range(parts)]
-
+    by_z = {j: at_z(j) for j in range(1, z_n)}
+    by_y = {j: at_y(j) for j in range(1, y_n)}
+    axes = ((z_n, z, by_z.get), (y_n, y, by_y.get))
+    first = [axes[p % 2] for p in range(parts)]
+    second = [axes[1 - p % 2] for p in range(parts)]
+
+    by_x = {j: at_x(j) for j in range(1, group)}
     for p in range(parts):
         for j in range(1, group):
-            to, a, b = at_x(j)
+            to, a, b = by_x[j]
             only(
                 to < count[p], count[p] == group,
                 functools.partial(pass_on, gbuf.at[p, to], rbuf.at[p, me], sem_rs, p, a, b),
             )
 
+    def hop(p, source, arrived, sem, held_as, axis, sems):
+        length, at, peer = axis
+
+        def go():
+            done(source.at[p], arrived - 1, sem.at[p])
+            held_as[p, at] = total(source, p, arrived)
+            for j in far_first(length):
+                pass_on(held_as.at[p, at], held_as.at[p, at], sems, p, *peer(j))
+
+        only(me < count[p], count[p] == group, go)
+
+    for p in range(parts):
+        def own(p=p):
+            rbuf[p, me] = gbuf[p, me]
+
+        only(me < count[p], count[p] == group, own)
+        hop(p, rbuf, group, sem_rs[1], ex1, first[p], sem_x1)
     sea = f_ref[CIN : CIN + 1, :].astype(F32)
     res = gather_rows(nn(wa2[...], hd[...]), ROWS) * sea
     for r in range(ROWS):
@@ -407,6 +430,10 @@
     c_in[...] = flip[: CH * ROWS, :].reshape(CH, ROWS, LANES).astype(BF)
     stores = [pltpu.make_async_copy(c_in, out_ref, in_sem.at[0])]
     stores[0].start()
+
+    for p in range(parts):
+        hop(p, ex1, first[p][0], sem_x1[1], ex2, second[p], sem_x2)
+
     v = jnp.concatenate(
         [nn(tb1[...], dad[:, tile(0, RIM - 1)]), nn(tb1n[...], dad[:, tile(RIM - 1)])], axis=1
     )
@@ -417,26 +444,7 @@
     stores.append(pltpu.make_async_copy(x_in, dx_ref, in_sem.at[1]))
     stores[1].start()
 
-    def hop(p, source, arrived, sem, held_as, axis, sems):
-        length, at, peer = axis
-
-        def go():
-            done(source.at[p], arrived - 1, sem.at[p])
-            held_as[p, at] = total(source, p, arrived)
-            for j in far_first(length):
-                pass_on(held_as.at[p, at], held_as.at[p, at], sems, p, *peer(j))
-
-        only(me < count[p], count[p] == group, go)
-
-    for p in range(parts):
-        def own(p=p):
-            rbuf[p, me] = gbuf[p, me]
-
-        only(me < count[p], count[p] == group, own)
-        hop(p, rbuf, group, sem_rs[1], ex1, first[p], sem_x1)
-    for p in range(parts):
-        hop(p, ex1, first[p][0], sem_x1[1], ex2, second[p], sem_x2)
-    everyone = (group, me, lambda j: at_x(j)[1:])
+    everyone = (group, me, lambda j: by_x[j][1:])
     for p in range(parts):
         hop(p, ex2, second[p][0], sem_x2[1], obuf, everyone, sem_ag)
     for p in range(parts):

time: 41.5 us -> 41.9 us (level)
  no operation moved by 1% of the time
where the time goes in v5:
time: 41.9 us; the launch traced here: 41.7 us
  Pallas kernels  41.1 us (98%)
  between operations  0.64 us (2%)
    pallas_call x1, Pallas kernels, body(): pl.pallas_call(functools.partial(kernel, dims), out_shape=fields_like + (...  39.9 us
    pallas_call x1, Pallas kernels, body(): pl.pallas_call(functools.partial(finish, factor, parts, group), out_shape...  1.17 us

profile of v5, /device:TPU:1, one launch (start us, length us, event | category | flops | bytes accessed | tf_op | source)
XLA Modules:
  0.0 41.7 jit_solution(6881548800162854938)
XLA Ops:
  0.6 39.9 %shard_map.84 = (bf16[48,8,128]{2,1,0:T(8,128)(2,1)S(1)}, bf16[75,8,128]{2,1,0:T(8,128)(2,1)S(1)}, bf16[4,8,16,128]{3,2,1,0:T(8,128)(2,1)S(1)}) custom-call(bf16[75,8,128]{2,1,0:T(8,128)(2,1)} %x_hbm.1, s32[8,128]{1,0:T(8,128)} %m_hbm.1, bf16[9,48,75]{2,1,0:T(8,128)(2,1)} %w1_hbm.1, bf16[9,48,48]{2,1,0:T(8,128)(2,1)} %w2_hbm.1, bf16[48,8,128]{2,1,0:T(8,128)(2,1)} %c_hbm.1), custom_call_target="tpu_custom_call" | custom-call | tf_op jit(solution)/shard_map/pallas_call | solution.py:563
  40.6 1.2 %shard_map.85 = (bf16[48,8,128]{2,1,0:T(8,128)(2,1)}, bf16[75,8,128]{2,1,0:T(8,128)(2,1)}, f32[9,48,75]{2,1,0:T(8,128)}, f32[9,48,48]{2,1,0:T(8,128)}) custom-call(bf16[48,8,128]{2,1,0:T(8,128)(2,1)S(1)} %get-tuple-element.7.out_in, bf16[75,8,128]{2,1,0:T(8,128)(2,1)S(1)} %get-tuple-element.8.dx_in, bf16[4,8,16,128]{3,2,1,0:T(8,128)(2,1)S(1)} %get-tuple-element.9.dw_in), custom_call_target="tpu_custom_call" | custom-call | tf_op jit(solution)/shard_map/pallas_call | solution.py:588

commit v6 on v5

--- a/solution.py
+++ b/solution.py
@@ -228,15 +228,18 @@
                 am[at, tile(r)] = zero
                 ae[at, tile(r)] = zero
 
-    k = lax.broadcasted_iota(jnp.int32, (96, 1), 0)
-    slot, row, j = k // 16, (k % 16) // 2, k % 2
-    row_to = jnp.where(slot < 2, row + 2, jnp.where(slot < 4, row + 10, row - 6))
-    row_to = jnp.where((slot >= 2) & (slot < 4) & top, 17 - row, row_to)
-    lane_to = jnp.where(slot % 2 == 0, LANES - 2 + j, j)
-    lane_to = jnp.where((slot == 2) & top, LANES - 1 - j, lane_to)
-    lane_to = jnp.where((slot == 3) & top, 1 - j, lane_to)
-    good = (slot < 2) | ((slot < 4) & (row_to < EXT)) | ((slot >= 4) & (row_to >= 0))
-    goal = jnp.where(good, row_to * LANES + lane_to, -1)
+    def select(cells, slot, tiles, base):
+        k = lax.broadcasted_iota(jnp.int32, (cells, 1), 0)
+        slot, row, j = slot(k // 16), (k % 16) // 2, k % 2
+        row_to = jnp.where(slot < 2, row + 2, jnp.where(slot < 4, row + 10, row - 6))
+        row_to = jnp.where((slot >= 2) & (slot < 4) & top, 17 - row, row_to)
+        lane_to = jnp.where(slot % 2 == 0, LANES - 2 + j, j)
+        lane_to = jnp.where((slot == 2) & top, LANES - 1 - j, lane_to)
+        lane_to = jnp.where((slot == 3) & top, 1 - j, lane_to)
+        good = (slot < 2) | ((slot < 4) & (row_to < EXT)) | ((slot >= 4) & (row_to >= 0))
+        goal = jnp.where(good, (row_to - base) * LANES + lane_to, -1)
+        place = lax.broadcasted_iota(jnp.int32, (cells, tiles * LANES), 1)
+        return (place == goal).astype(F32).astype(BF)
 
     loads[3].wait()
     loads[4].wait()
@@ -275,45 +278,6 @@
     def landed(ref, slot):
         pltpu.make_async_copy(ref, ref, recv_sem.at[slot]).wait()
 
-    landed(packs.at[0], 0)
-    landed(packs.at[1], 1)
-
-    @pl.when(jnp.logical_not(top))
-    def _():
-        landed(above, 8)
-        landed(packs.at[2], 2)
-        landed(packs.at[3], 3)
-
-    @pl.when(top)
-    def _():
-        landed(above, 6)
-
-        @pl.when(fold_e != lon)
-        def _():
-            landed(packs.at[3], 9)
-
-        @pl.when(fold_w != lon)
-        def _():
-            landed(packs.at[2], 10)
-
-        back = lax.broadcasted_iota(jnp.int32, (LANES, LANES), 0)
-        back = back + lax.broadcasted_iota(jnp.int32, (LANES, LANES), 1)
-        back = (back == LANES - 1).astype(F32).astype(BF)
-        first = nn(xm[:, tile(ROWS + 2)], back).astype(BF)
-        second = nn(xm[:, tile(ROWS + 3)], back).astype(BF)
-        xm[:, tile(ROWS + 2)] = second
-        xm[:, tile(ROWS + 3)] = first
-
-    @pl.when(jnp.logical_not(bottom))
-    def _():
-        landed(below, 7)
-        landed(packs.at[4], 4)
-        landed(packs.at[5], 5)
-
-    flat = jnp.concatenate([packs[s] for s in range(6)], axis=0)
-    lanes96 = lax.broadcasted_iota(jnp.int32, (96, EXT * LANES), 1)
-    xg[...] = tn(flat, (lanes96 == goal).astype(F32).astype(BF)).astype(BF)
-
     lane = lax.broadcasted_iota(jnp.int32, (1, LANES), 1)
 
     def shifts(main, ghost):
@@ -326,42 +290,116 @@
         gb = jnp.where(lane == LANES - 1, right[0], right[1]).astype(BF)
         return a, b, ga, gb
 
-    for r in range(EXT):
-        t = tile(r)
-        main, ghost = xm[:, t], xg[:, t]
-        a, b, ga, gb = shifts(main, ghost)
-        for q, m, g in ((0, a, ga), (1, main, ghost), (2, b, gb)):
-            d1m[q * KX : (q + 1) * KX, t] = m[:KX]
-            d1g[q * KX : (q + 1) * KX, t] = g[:KX]
-            d2m[q * CH : (q + 1) * CH, t] = m[KX:]
-            d2g[q * CH : (q + 1) * CH, t] = g[KX:]
-
-    def hidden(d1, d2, field):
-        a = gather_rows(nn(wa1[...], d1[...]), RIM)
-        last = gather_rows(nn(wa1n[...], d1[:, tile(RIM - 1, 3)]), 1)
-        a = jnp.concatenate([a[:, : (RIM - 1) * LANES], last], axis=1)
+    def spread(rows):
+        for r in rows:
+            t = tile(r)
+            main, ghost = xm[:, t], xg[:, t]
+            a, b, ga, gb = shifts(main, ghost)
+            for q, m, g in ((0, a, ga), (1, main, ghost), (2, b, gb)):
+                d1m[q * KX : (q + 1) * KX, t] = m[:KX]
+                d1g[q * KX : (q + 1) * KX, t] = g[:KX]
+                d2m[q * CH : (q + 1) * CH, t] = m[KX:]
+                d2g[q * CH : (q + 1) * CH, t] = g[KX:]
+
+    def spread_results(h, g, base):
+        for r in range(h[0].shape[1] // LANES):
+            t, to = tile(r), tile(base + r)
+            for ref, (main, ghost) in ((hd, h), (dad, g)):
+                main = main[:, t]
+                a, b, _, _ = shifts(main, ghost[:, t])
+                ref[0:CH, to] = a
+                ref[CH : 2 * CH, to] = main
+                ref[2 * CH :, to] = b
+
+    def gated(a, grad, field, t):
         value, slope = gelu_parts(a)
-        sea = field[CIN : CIN + 1, tile(1, RIM)].astype(F32)
-        z = jnp.concatenate(
-            [nn(tb2[...], d2[:, tile(0, RIM)]), nn(tb2n[...], d2[:, tile(RIM, 2)])], axis=1
+        sea = field[CIN : CIN + 1, t].astype(F32)
+        return (value * sea).astype(BF), (grad * (slope * sea)).astype(BF)
+
+    inner = RIM - 2
+
+    def lower(d1, d2, field):
+        y = nn(wa1[...], d1[:, tile(0, RIM)])
+        v = nn(tb2[...], d2[:, tile(0, RIM)])
+        left = tuple(
+            u[:CH, tile(inner)] + u[CH : 2 * CH, tile(inner + 1)] for u in (y, v)
+        ) + (v[:CH, tile(inner + 1)],)
+        h, g = gated(gather_rows(y, inner), gather_rows(v, inner), field, tile(1, inner))
+        return h, g, left
+
+    def upper(d1, d2, field, left):
+        y = nn(wa1[...], d1[:, tile(RIM)])
+        yn = nn(wa1n[...], d1[:, tile(RIM - 1, 3)])
+        v = nn(tb2n[...], d2[:, tile(RIM, 2)])
+        a = jnp.concatenate([left[0] + y[2 * CH :], gather_rows(yn, 1)], axis=1)
+        grad = jnp.concatenate(
+            [
+                left[1] + v[2 * CH :, tile(0)],
+                left[2] + v[CH : 2 * CH, tile(0)] + v[2 * CH :, tile(1)],
+            ],
+            axis=1,
         )
-        grad = (gather_rows(z, RIM) * (slope * sea)).astype(BF)
-        return (value * sea).astype(BF), grad
-
-    hm, gm = hidden(d1m, d2m, xm)
-    hg, gg = hidden(d1g, d2g, xg)
+        return gated(a, grad, field, tile(RIM - 1, 2))
+
+    pick_low = select(64, lambda s: jnp.where(s < 2, s, s + 2), RIM, 0)
+    pick_high = select(32, lambda s: s + 2, 2, RIM)
+
+    landed(packs.at[0], 0)
+    landed(packs.at[1], 1)
+
+    @pl.when(jnp.logical_not(bottom))
+    def _():
+        landed(below, 7)
+        landed(packs.at[4], 4)
+        landed(packs.at[5], 5)
+
+    flat = jnp.concatenate([packs[s] for s in (0, 1, 4, 5)], axis=0)
+    xg[:, tile(0, RIM)] = tn(flat, pick_low).astype(BF)
+    spread(range(RIM))
+    hm, gm, left_m = lower(d1m, d2m, xm)
+    hg, gg, left_g = lower(d1g, d2g, xg)
     for dr in range(3):
-        am[dr * CH : (dr + 1) * CH, tile(dr, ROWS)] = gm[:, tile(1, ROWS)]
-    for r in range(RIM):
-        t = tile(r)
-        for ref, main, ghost in ((hd, hm[:, t], hg[:, t]), (dad, gm[:, t], gg[:, t])):
-            a, b, _, _ = shifts(main, ghost)
-            ref[0:CH, t] = a
-            ref[CH : 2 * CH, t] = main
-            ref[2 * CH :, t] = b
-
-    term2 = nt(ae[...], hd[...])
-    term1 = nt(am[...], d1m[:, tile(1, RIM)])
+        am[dr * CH : (dr + 1) * CH, tile(dr, ROWS - 1)] = gm[:, tile(1, ROWS - 1)]
+    spread_results((hm, hg), (gm, gg), 0)
+    term2 = nt(ae[:, tile(0, inner)], hd[:, tile(0, inner)])
+    term1 = nt(am[:, tile(0, inner - 1)], d1m[:, tile(1, inner - 1)])
+
+    @pl.when(jnp.logical_not(top))
+    def _():
+        landed(above, 8)
+        landed(packs.at[2], 2)
+        landed(packs.at[3], 3)
+
+    @pl.when(top)
+    def _():
+        landed(above, 6)
+
+        @pl.when(fold_e != lon)
+        def _():
+            landed(packs.at[3], 9)
+
+        @pl.when(fold_w != lon)
+        def _():
+            landed(packs.at[2], 10)
+
+        back = lax.broadcasted_iota(jnp.int32, (LANES, LANES), 0)
+        back = back + lax.broadcasted_iota(jnp.int32, (LANES, LANES), 1)
+        back = (back == LANES - 1).astype(F32).astype(BF)
+        first = nn(xm[:, tile(ROWS + 2)], back).astype(BF)
+        second = nn(xm[:, tile(ROWS + 3)], back).astype(BF)
+        xm[:, tile(ROWS + 2)] = second
+        xm[:, tile(ROWS + 3)] = first
+
+    flat = jnp.concatenate([packs[s] for s in (2, 3)], axis=0)
+    xg[:, tile(RIM, 2)] = tn(flat, pick_high).astype(BF)
+    spread((RIM, RIM + 1))
+    hm, gm = upper(d1m, d2m, xm, left_m)
+    hg, gg = upper(d1g, d2g, xg, left_g)
+    for dr in range(3):
+        am[dr * CH : (dr + 1) * CH, tile(dr + ROWS - 1)] = gm[:, tile(0)]
+    spread_results((hm, hg), (gm, gg), inner)
+    term2 = term2 + nt(ae[:, tile(inner, 2)], hd[:, tile(inner, 2)])
+    term1 = term1 + nt(am[:, tile(inner - 1, 3)], d1m[:, tile(inner, 3)])
     terms = jnp.concatenate([term1, term2], axis=1).astype(BF)
     for t in range(TILES):
         a, b = t // 3, t % 3

time: 41.9 us -> 41.8 us (level)
  no operation moved by 1% of the time
where the time goes in v6:
time: 41.8 us; the launch traced here: 41.7 us
  Pallas kernels  41 us (98%)
  between operations  0.64 us (2%)
    pallas_call x1, Pallas kernels, body(): pl.pallas_call(functools.partial(kernel, dims), out_shape=fields_like + (...  39.8 us
    pallas_call x1, Pallas kernels, body(): pl.pallas_call(functools.partial(finish, factor, parts, group), out_shape...  1.17 us

profile of v6, /device:TPU:1, one launch (start us, length us, event | category | flops | bytes accessed | tf_op | source)
XLA Modules:
  0.0 41.7 jit_solution(16730657742906676429)
XLA Ops:
  0.6 39.8 %shard_map.84 = (bf16[48,8,128]{2,1,0:T(8,128)(2,1)S(1)}, bf16[75,8,128]{2,1,0:T(8,128)(2,1)S(1)}, bf16[4,8,16,128]{3,2,1,0:T(8,128)(2,1)S(1)}) custom-call(bf16[75,8,128]{2,1,0:T(8,128)(2,1)} %x_hbm.1, s32[8,128]{1,0:T(8,128)} %m_hbm.1, bf16[9,48,75]{2,1,0:T(8,128)(2,1)} %w1_hbm.1, bf16[9,48,48]{2,1,0:T(8,128)(2,1)} %w2_hbm.1, bf16[48,8,128]{2,1,0:T(8,128)(2,1)} %c_hbm.1), custom_call_target="tpu_custom_call" | custom-call | tf_op jit(solution)/shard_map/pallas_call | solution.py:601
  40.5 1.2 %shard_map.85 = (bf16[48,8,128]{2,1,0:T(8,128)(2,1)}, bf16[75,8,128]{2,1,0:T(8,128)(2,1)}, f32[9,48,75]{2,1,0:T(8,128)}, f32[9,48,48]{2,1,0:T(8,128)}) custom-call(bf16[48,8,128]{2,1,0:T(8,128)(2,1)S(1)} %get-tuple-element.7.out_in, bf16[75,8,128]{2,1,0:T(8,128)(2,1)S(1)} %get-tuple-element.8.dx_in, bf16[4,8,16,128]{3,2,1,0:T(8,128)(2,1)S(1)} %get-tuple-element.9.dw_in), custom_call_target="tpu_custom_call" | custom-call | tf_op jit(solution)/shard_map/pallas_call | solution.py:626

commit v7 on v6

--- a/solution.py
+++ b/solution.py
@@ -16,6 +16,9 @@
 EXT = ROWS + 4
 RIM = ROWS + 2
 TILES = 27
+UNIT = 2
+CHUNKS = -(-TILES // UNIT)
+TALL = 16 * UNIT
 
 
 def nn(a, b):
@@ -49,6 +52,11 @@
     return y[:c, :n] + y[c : 2 * c, LANES : LANES + n] + y[2 * c :, 2 * LANES : 2 * LANES + n]
 
 
+def chunk_of(t, group):
+    c, row = t // UNIT, t % UNIT * 16
+    return c // group, c % group, slice(row, row + 16)
+
+
 def far_first(n):
     return sorted(range(1, n), key=lambda j: -min(j, n - j))
 
@@ -56,11 +64,11 @@
 def kernel(
     dims,
     x_hbm, m_hbm, w1_hbm, w2_hbm, c_hbm,
-    out_ref, dx_ref, dw_ref,
+    out_ref, dx_ref, dw1_ref, dw2_ref,
     x_in, m_in, w1_in, w2_in, c_in, flip, f_ref,
     wa1, wa1n, wa2, tb2, tb2n, tb1, tb1n,
     xm, xg, packs, mine, d1m, d1g, d2m, d2g, hd, dad, am, ae,
-    gbuf, rbuf, ex1, ex2, obuf,
+    gbuf, rbuf, ex1, ex2, obuf, dw1, dw2,
     in_sem, out_sem, send_sem, recv_sem, *red,
 ):
     sem_rs, sem_x1, sem_x2, sem_ag = red[0:2], red[2:4], red[4:6], red[6:8]
@@ -84,10 +92,14 @@
         to = lax.rem(y + j, y_n)
         return lat, (xh * y_n + to) * c_n + core
 
-    def at_x(j):
-        to = lax.rem(me + j, group)
-        a, b, c = to // (xh_n * c_n), (to // c_n) % xh_n, to % c_n
-        return to, a * z_n + z, (b * y_n + y) * c_n + c
+    def at_x(d):
+        a, b, c = lax.rem(xl + d[0], xl_n), lax.rem(xh + d[1], xh_n), lax.rem(core + d[2], c_n)
+        return (a * xh_n + b) * c_n + c, a * z_n + z, (b * y_n + y) * c_n + c
+
+    others = [
+        (a, b, c) for a in range(xl_n) for b in range(xh_n) for c in range(c_n) if a or b or c
+    ]
+    others.sort(key=lambda d: 0 if d[1] and not d[0] else 1 if d[0] else 2)
 
     loads = [
         pltpu.make_async_copy(src, dst, in_sem.at[i])
@@ -119,8 +131,8 @@
         greet(*at_y(j))
     for j in far_first(z_n):
         greet(*at_z(j))
-    for j in range(1, group):
-        greet(*at_x(j)[1:])
+    for d in others:
+        greet(*at_x(d)[1:])
 
     @pl.when(jnp.logical_not(top))
     def _():
@@ -403,7 +415,9 @@
     terms = jnp.concatenate([term1, term2], axis=1).astype(BF)
     for t in range(TILES):
         a, b = t // 3, t % 3
-        gbuf[t // group, t % group] = terms[16 * a : 16 * a + 16, tile(b)]
+        gbuf[chunk_of(t, group)] = terms[16 * a : 16 * a + 16, tile(b)]
+    for t in range(TILES, CHUNKS * UNIT):
+        gbuf[chunk_of(t, group)] = jnp.zeros((16, LANES), BF)
 
     def pass_on(src, dst, sems, p, a, b):
         pltpu.make_async_remote_copy(
@@ -427,30 +441,30 @@
         else:
             pl.when(test)(f)
 
-    parts = -(-TILES // group)
-    count = [min(group, TILES - p * group) for p in range(parts)]
+    parts = -(-CHUNKS // group)
+    count = [min(group, CHUNKS - p * group) for p in range(parts)]
     by_z = {j: at_z(j) for j in range(1, z_n)}
     by_y = {j: at_y(j) for j in range(1, y_n)}
-    axes = ((z_n, z, by_z.get), (y_n, y, by_y.get))
+    axes = ((z_n, z, far_first(z_n), by_z.get), (y_n, y, far_first(y_n), by_y.get))
     first = [axes[p % 2] for p in range(parts)]
     second = [axes[1 - p % 2] for p in range(parts)]
 
-    by_x = {j: at_x(j) for j in range(1, group)}
+    by_x = {d: at_x(d) for d in others}
     for p in range(parts):
-        for j in range(1, group):
-            to, a, b = by_x[j]
+        for d in others:
+            to, a, b = by_x[d]
             only(
                 to < count[p], count[p] == group,
                 functools.partial(pass_on, gbuf.at[p, to], rbuf.at[p, me], sem_rs, p, a, b),
             )
 
     def hop(p, source, arrived, sem, held_as, axis, sems):
-        length, at, peer = axis
+        _, at, order, peer = axis
 
         def go():
             done(source.at[p], arrived - 1, sem.at[p])
             held_as[p, at] = total(source, p, arrived)
-            for j in far_first(length):
+            for j in order:
                 pass_on(held_as.at[p, at], held_as.at[p, at], sems, p, *peer(j))
 
         only(me < count[p], count[p] == group, go)
@@ -482,7 +496,7 @@
     stores.append(pltpu.make_async_copy(x_in, dx_ref, in_sem.at[1]))
     stores[1].start()
 
-    everyone = (group, me, lambda j: by_x[j][1:])
+    everyone = (group, me, others, lambda d: by_x[d][1:])
     for p in range(parts):
         hop(p, ex2, second[p][0], sem_x2[1], obuf, everyone, sem_ag)
     for p in range(parts):
@@ -495,10 +509,23 @@
             pl.when(me >= count[p])(
                 functools.partial(done, obuf.at[p], count[p], sem_ag[1].at[p])
             )
-        n = count[p]
-        move = pltpu.make_async_copy(obuf.at[p, pl.ds(0, n)], dw_ref.at[p, pl.ds(0, n)], out_sem.at[p])
-        move.start()
-        stores.append(move)
+
+    for dr in range(3):
+        grads = jnp.concatenate(
+            [
+                jnp.concatenate(
+                    [obuf[chunk_of(t, group)] for t in range(3 * a, 3 * a + 3)], axis=1
+                )
+                for a in range(3 * dr, 3 * dr + 3)
+            ],
+            axis=0,
+        ).astype(F32) * (1.0 / math.sqrt(ROWS * LANES * nlat * nlon))
+        for dc in range(3):
+            dw1[3 * dr + dc] = grads[:, dc * KX : dc * KX + CIN]
+            dw2[3 * dr + dc] = grads[:, 3 * KX + dc * CH : 3 * KX + (dc + 1) * CH]
+    for i, (src, dst) in enumerate(((dw1, dw1_ref), (dw2, dw2_ref))):
+        stores.append(pltpu.make_async_copy(src, dst, out_sem.at[i]))
+        stores[-1].start()
 
     def sent(ref, sem):
         pltpu.make_async_copy(ref, ref, sem).wait()
@@ -548,45 +575,21 @@
         store.wait()
 
 
-def finish(
-    factor, parts, group,
-    out_in, dx_in, dw_in, out_ref, dx_ref, dw1_ref, dw2_ref,
-    tiles, dw1, dw2, get_sem, put_sem,
-):
-    get = pltpu.make_async_copy(dw_in, tiles, get_sem)
-    puts = [
-        pltpu.make_async_copy(src, dst, put_sem.at[i])
-        for i, (src, dst) in enumerate(
-            ((dw1, dw1_ref), (dw2, dw2_ref), (out_in, out_ref), (dx_in, dx_ref))
-        )
+def finish(*refs):
+    moves = [
+        pltpu.make_async_copy(src, dst, refs[8].at[i])
+        for i, (src, dst) in enumerate(zip(refs[:4], refs[4:8]))
     ]
-    get.start()
-    puts[2].start()
-    puts[3].start()
-    get.wait()
-    for dr in range(3):
-        grads = jnp.concatenate(
-            [
-                jnp.concatenate(
-                    [tiles[t // group, t % group] for t in range(3 * a, 3 * a + 3)], axis=1
-                )
-                for a in range(3 * dr, 3 * dr + 3)
-            ],
-            axis=0,
-        ).astype(F32) * factor
-        for dc in range(3):
-            dw1[3 * dr + dc] = grads[:, dc * KX : dc * KX + CIN]
-            dw2[3 * dr + dc] = grads[:, 3 * KX + dc * CH : 3 * KX + (dc + 1) * CH]
-    puts[0].start()
-    puts[1].start()
-    for put in puts:
-        put.wait()
+    for move in moves:
+        move.start()
+    for move in moves:
+        move.wait()
 
 
 def body(dims, *inputs):
     xl_n, z_n, xh_n, y_n, c_n = dims
     group = xl_n * xh_n * c_n
-    parts = -(-TILES // group)
+    parts = -(-CHUNKS // group)
     wide, slim, ring = EXT * LANES, RIM * LANES, max(y_n, z_n)
     anywhere = pl.BlockSpec(memory_space=pl.ANY)
     hbm = pl.BlockSpec(memory_space=pltpu.HBM)
@@ -594,15 +597,17 @@
     def held(*shape):
         return pltpu.VMEM(shape, BF)
 
-    fields_like = (
+    results = (
         jax.ShapeDtypeStruct((CH, ROWS, LANES), BF),
         jax.ShapeDtypeStruct((CIN, ROWS, LANES), BF),
+        jax.ShapeDtypeStruct((9, CH, CIN), F32),
+        jax.ShapeDtypeStruct((9, CH, CH), F32),
     )
-    out, dx, dw = pl.pallas_call(
+    held_results = pl.pallas_call(
         functools.partial(kernel, dims),
-        out_shape=fields_like + (jax.ShapeDtypeStruct((parts, group, 16, LANES), BF),),
+        out_shape=results,
         in_specs=[hbm] * 5,
-        out_specs=(anywhere,) * 3,
+        out_specs=(anywhere,) * 4,
         scratch_shapes=[
             held(CIN, ROWS, LANES), pltpu.VMEM((ROWS, LANES), jnp.int32),
             held(9, CH, CIN), held(9, CH, CH), held(CH, ROWS, LANES),
@@ -612,32 +617,25 @@
             held(128, wide), held(128, wide), held(6, 16, 128), held(2, 16, 128),
             held(3 * KX, wide), held(3 * KX, wide), held(3 * CH, wide), held(3 * CH, wide),
             held(3 * CH, slim), held(3 * CH, slim), held(3 * CH, slim), held(3 * CH, slim),
-            held(parts, group, 16, LANES), held(parts, group, 16, LANES),
-            held(parts, ring, 16, LANES), held(parts, ring, 16, LANES),
-            held(parts, group, 16, LANES),
-            pltpu.SemaphoreType.DMA((5,)), pltpu.SemaphoreType.DMA((parts,)),
+            held(parts, group, TALL, LANES), held(parts, group, TALL, LANES),
+            held(parts, ring, TALL, LANES), held(parts, ring, TALL, LANES),
+            held(parts, group, TALL, LANES),
+            pltpu.VMEM((9, CH, CIN), F32), pltpu.VMEM((9, CH, CH), F32),
+            pltpu.SemaphoreType.DMA((5,)), pltpu.SemaphoreType.DMA((2,)),
             pltpu.SemaphoreType.DMA((11,)), pltpu.SemaphoreType.DMA((11,)),
         ] + [pltpu.SemaphoreType.DMA((parts,))] * 8,
         compiler_params=pltpu.CompilerParams(
             collective_id=0, has_side_effects=True, vmem_limit_bytes=24 * 1024 * 1024
         ),
     )(*(pltpu.with_memory_space_constraint(v, pltpu.HBM) for v in inputs))
-    factor = 1.0 / math.sqrt(ROWS * LANES * xl_n * z_n * xh_n * y_n * c_n)
     return pl.pallas_call(
-        functools.partial(finish, factor, parts, group),
-        out_shape=fields_like + (
-            jax.ShapeDtypeStruct((9, CH, CIN), F32),
-            jax.ShapeDtypeStruct((9, CH, CH), F32),
-        ),
-        in_specs=[anywhere] * 3,
+        finish,
+        out_shape=results,
+        in_specs=[anywhere] * 4,
         out_specs=(hbm,) * 4,
-        scratch_shapes=[
-            held(parts, group, 16, LANES),
-            pltpu.VMEM((9, CH, CIN), F32), pltpu.VMEM((9, CH, CH), F32),
-            pltpu.SemaphoreType.DMA, pltpu.SemaphoreType.DMA((4,)),
-        ],
+        scratch_shapes=[pltpu.SemaphoreType.DMA((4,))],
         compiler_params=pltpu.CompilerParams(vmem_limit_bytes=8 * 1024 * 1024),
-    )(out, dx, dw)
+    )(*held_results)
 
 
 def solution(mesh):

time: 41.8 us -> 42.5 us (1.017)
  Pallas kernels: 41 us -> 41.7 us
    pallas_call x2, Pallas kernels: 41 us -> 41.7 us  [the longest x1 40.8 us: body(): pl.pallas_call(functools.partial(kernel, dims), out_shape=results, in_spe...]
where the time goes in v7:
time: 42.5 us; the launch traced here: 42.4 us
  Pallas kernels  41.7 us (98%)
  between operations  0.64 us (2%)
    pallas_call x1, Pallas kernels, body(): pl.pallas_call(functools.partial(kernel, dims), out_shape=results, in_spe...  40.8 us
    pallas_call x1, Pallas kernels, body(): pl.pallas_call(finish, out_shape=results, in_specs=[anywhere] * 4, out_sp...  0.88 us

profile of v7, /device:TPU:1, one launch (start us, length us, event | category | flops | bytes accessed | tf_op | source)
XLA Modules:
  0.0 42.4 jit_solution(6885829721615897875)
XLA Ops:
  0.6 40.8 %shard_map.84 = (bf16[48,8,128]{2,1,0:T(8,128)(2,1)S(1)}, bf16[75,8,128]{2,1,0:T(8,128)(2,1)S(1)}, f32[9,48,75]{2,1,0:T(8,128)S(1)}, f32[9,48,48]{2,1,0:T(8,128)S(1)}) custom-call(bf16[75,8,128]{2,1,0:T(8,128)(2,1)} %x_hbm.1, s32[8,128]{1,0:T(8,128)} %m_hbm.1, bf16[9,48,75]{2,1,0:T(8,128)(2,1)} %w1_hbm.1, bf16[9,48,48]{2,1,0:T(8,128)(2,1)} %w2_hbm.1, ...), custom_call_target="tpu_custom_call" | custom-call | tf_op jit(solution)/shard_map/pallas_call | solution.py:606
  41.5 0.9 %shard_map.85 = (bf16[48,8,128]{2,1,0:T(8,128)(2,1)}, bf16[75,8,128]{2,1,0:T(8,128)(2,1)}, f32[9,48,75]{2,1,0:T(8,128)}, f32[9,48,48]{2,1,0:T(8,128)}) custom-call(bf16[48,8,128]{2,1,0:T(8,128)(2,1)S(1)} %get-tuple-element.8.refs_0_, bf16[75,8,128]{2,1,0:T(8,128)(2,1)S(1)} %get-tuple-element.9.refs_1_, f32[9,48,75]{2,1,0:T(8,128)S(1)} %get-tuple-element.10.refs_2_, ...), custom_call_target="tpu_custom_call" | custom-call | tf_op jit(solution)/shard_map/pallas_call | solution.py:631

commit v8 on v6

--- a/solution.py
+++ b/solution.py
@@ -16,6 +16,9 @@
 EXT = ROWS + 4
 RIM = ROWS + 2
 TILES = 27
+UNIT = 2
+CHUNKS = -(-TILES // UNIT)
+TALL = 16 * UNIT
 
 
 def nn(a, b):
@@ -49,6 +52,11 @@
     return y[:c, :n] + y[c : 2 * c, LANES : LANES + n] + y[2 * c :, 2 * LANES : 2 * LANES + n]
 
 
+def chunk_of(t, group):
+    c, row = t // UNIT, t % UNIT * 16
+    return c // group, c % group, slice(row, row + 16)
+
+
 def far_first(n):
     return sorted(range(1, n), key=lambda j: -min(j, n - j))
 
@@ -59,7 +67,7 @@
     out_ref, dx_ref, dw_ref,
     x_in, m_in, w1_in, w2_in, c_in, flip, f_ref,
     wa1, wa1n, wa2, tb2, tb2n, tb1, tb1n,
-    xm, xg, packs, mine, d1m, d1g, d2m, d2g, hd, dad, am, ae,
+    xm, xg, xo, packs, mine, d1m, d1g, d2m, d2g, hd, dad, am, ae,
     gbuf, rbuf, ex1, ex2, obuf,
     in_sem, out_sem, send_sem, recv_sem, *red,
 ):
@@ -115,27 +123,27 @@
         def _():
             greet(lat, fold_w)
 
+    @pl.when(jnp.logical_not(top))
+    def _():
+        greet(lat + 1, east)
+        greet(lat + 1, west)
+        greet(lat + 1, lon)
+
+    @pl.when(jnp.logical_not(bottom))
+    def _():
+        greet(lat - 1, east)
+        greet(lat - 1, west)
+        greet(lat - 1, lon)
+
+    greet(lat, east)
+    greet(lat, west)
+
     for j in far_first(y_n):
         greet(*at_y(j))
     for j in far_first(z_n):
         greet(*at_z(j))
     for j in range(1, group):
         greet(*at_x(j)[1:])
-
-    @pl.when(jnp.logical_not(top))
-    def _():
-        greet(lat + 1, east)
-        greet(lat + 1, west)
-        greet(lat + 1, lon)
-
-    @pl.when(jnp.logical_not(bottom))
-    def _():
-        greet(lat - 1, east)
-        greet(lat - 1, west)
-        greet(lat - 1, lon)
-
-    greet(lat, east)
-    greet(lat, west)
 
     for load in loads[:3]:
         load.wait()
@@ -233,12 +241,13 @@
         slot, row, j = slot(k // 16), (k % 16) // 2, k % 2
         row_to = jnp.where(slot < 2, row + 2, jnp.where(slot < 4, row + 10, row - 6))
         row_to = jnp.where((slot >= 2) & (slot < 4) & top, 17 - row, row_to)
-        lane_to = jnp.where(slot % 2 == 0, LANES - 2 + j, j)
-        lane_to = jnp.where((slot == 2) & top, LANES - 1 - j, lane_to)
-        lane_to = jnp.where((slot == 3) & top, 1 - j, lane_to)
+        flipped = (slot >= 2) & (slot < 4) & top
+        inner = (j + slot + jnp.where(flipped, 1, 0)) % 2 == 1
+        lane_to = jnp.where(slot % 2 == 0, 0, LANES - 1)
         good = (slot < 2) | ((slot < 4) & (row_to < EXT)) | ((slot >= 4) & (row_to >= 0))
-        goal = jnp.where(good, (row_to - base) * LANES + lane_to, -1)
-        place = lax.broadcasted_iota(jnp.int32, (cells, tiles * LANES), 1)
+        tile_to = row_to - base + jnp.where(inner, 0, tiles)
+        goal = jnp.where(good, tile_to * LANES + lane_to, -1)
+        place = lax.broadcasted_iota(jnp.int32, (cells, 2 * tiles * LANES), 1)
         return (place == goal).astype(F32).astype(BF)
 
     loads[3].wait()
@@ -282,19 +291,17 @@
 
     def shifts(main, ghost):
         main, ghost = main.astype(F32), ghost.astype(F32)
-        left = (pltpu.roll(main, 1, 1), pltpu.roll(ghost, 1, 1))
-        right = (pltpu.roll(main, LANES - 1, 1), pltpu.roll(ghost, LANES - 1, 1))
-        a = jnp.where(lane == 0, left[1], left[0]).astype(BF)
-        b = jnp.where(lane == LANES - 1, right[1], right[0]).astype(BF)
-        ga = jnp.where(lane == 0, left[0], left[1]).astype(BF)
-        gb = jnp.where(lane == LANES - 1, right[0], right[1]).astype(BF)
-        return a, b, ga, gb
+        a = jnp.where(lane == 0, ghost, pltpu.roll(main, 1, 1)).astype(BF)
+        b = jnp.where(lane == LANES - 1, ghost, pltpu.roll(main, LANES - 1, 1)).astype(BF)
+        return a, b
 
     def spread(rows):
         for r in rows:
             t = tile(r)
-            main, ghost = xm[:, t], xg[:, t]
-            a, b, ga, gb = shifts(main, ghost)
+            main, ghost, far = xm[:, t], xg[:, t], xo[:, t]
+            a, b = shifts(main, ghost)
+            ga = jnp.where(lane == LANES - 1, main, far)
+            gb = jnp.where(lane == 0, main, far)
             for q, m, g in ((0, a, ga), (1, main, ghost), (2, b, gb)):
                 d1m[q * KX : (q + 1) * KX, t] = m[:KX]
                 d1g[q * KX : (q + 1) * KX, t] = g[:KX]
@@ -306,7 +313,7 @@
             t, to = tile(r), tile(base + r)
             for ref, (main, ghost) in ((hd, h), (dad, g)):
                 main = main[:, t]
-                a, b, _, _ = shifts(main, ghost[:, t])
+                a, b = shifts(main, ghost[:, t])
                 ref[0:CH, to] = a
                 ref[CH : 2 * CH, to] = main
                 ref[2 * CH :, to] = b
@@ -354,7 +361,9 @@
         landed(packs.at[5], 5)
 
     flat = jnp.concatenate([packs[s] for s in (0, 1, 4, 5)], axis=0)
-    xg[:, tile(0, RIM)] = tn(flat, pick_low).astype(BF)
+    edge = tn(flat, pick_low).astype(BF)
+    xg[:, tile(0, RIM)] = edge[:, tile(0, RIM)]
+    xo[:, tile(0, RIM)] = edge[:, tile(RIM, RIM)]
     spread(range(RIM))
     hm, gm, left_m = lower(d1m, d2m, xm)
     hg, gg, left_g = lower(d1g, d2g, xg)
@@ -391,7 +400,9 @@
         xm[:, tile(ROWS + 3)] = first
 
     flat = jnp.concatenate([packs[s] for s in (2, 3)], axis=0)
-    xg[:, tile(RIM, 2)] = tn(flat, pick_high).astype(BF)
+    edge = tn(flat, pick_high).astype(BF)
+    xg[:, tile(RIM, 2)] = edge[:, tile(0, 2)]
+    xo[:, tile(RIM, 2)] = edge[:, tile(2, 2)]
     spread((RIM, RIM + 1))
     hm, gm = upper(d1m, d2m, xm, left_m)
     hg, gg = upper(d1g, d2g, xg, left_g)
@@ -403,7 +414,9 @@
     terms = jnp.concatenate([term1, term2], axis=1).astype(BF)
     for t in range(TILES):
         a, b = t // 3, t % 3
-        gbuf[t // group, t % group] = terms[16 * a : 16 * a + 16, tile(b)]
+        gbuf[chunk_of(t, group)] = terms[16 * a : 16 * a + 16, tile(b)]
+    for t in range(TILES, CHUNKS * UNIT):
+        gbuf[chunk_of(t, group)] = jnp.zeros((16, LANES), BF)
 
     def pass_on(src, dst, sems, p, a, b):
         pltpu.make_async_remote_copy(
@@ -427,8 +440,8 @@
         else:
             pl.when(test)(f)
 
-    parts = -(-TILES // group)
-    count = [min(group, TILES - p * group) for p in range(parts)]
+    parts = -(-CHUNKS // group)
+    count = [min(group, CHUNKS - p * group) for p in range(parts)]
     by_z = {j: at_z(j) for j in range(1, z_n)}
     by_y = {j: at_y(j) for j in range(1, y_n)}
     axes = ((z_n, z, by_z.get), (y_n, y, by_y.get))
@@ -568,7 +581,7 @@
         grads = jnp.concatenate(
             [
                 jnp.concatenate(
-                    [tiles[t // group, t % group] for t in range(3 * a, 3 * a + 3)], axis=1
+                    [tiles[chunk_of(t, group)] for t in range(3 * a, 3 * a + 3)], axis=1
                 )
                 for a in range(3 * dr, 3 * dr + 3)
             ],
@@ -586,7 +599,7 @@
 def body(dims, *inputs):
     xl_n, z_n, xh_n, y_n, c_n = dims
     group = xl_n * xh_n * c_n
-    parts = -(-TILES // group)
+    parts = -(-CHUNKS // group)
     wide, slim, ring = EXT * LANES, RIM * LANES, max(y_n, z_n)
     anywhere = pl.BlockSpec(memory_space=pl.ANY)
     hbm = pl.BlockSpec(memory_space=pltpu.HBM)
@@ -600,7 +613,7 @@
     )
     out, dx, dw = pl.pallas_call(
         functools.partial(kernel, dims),
-        out_shape=fields_like + (jax.ShapeDtypeStruct((parts, group, 16, LANES), BF),),
+        out_shape=fields_like + (jax.ShapeDtypeStruct((parts, group, TALL, LANES), BF),),
         in_specs=[hbm] * 5,
         out_specs=(anywhere,) * 3,
         scratch_shapes=[
@@ -609,12 +622,12 @@
             pltpu.VMEM(((KX + CH) * ROWS, LANES), F32), held(KX + CH, ROWS * LANES),
             held(3 * CH, 3 * KX), held(3 * CH, 3 * KX), held(3 * CH, 3 * CH),
             held(3 * CH, 3 * CH), held(3 * CH, 3 * CH), held(3 * KX, 3 * CH), held(3 * KX, 3 * CH),
-            held(128, wide), held(128, wide), held(6, 16, 128), held(2, 16, 128),
+            held(128, wide), held(128, wide), held(128, wide), held(6, 16, 128), held(2, 16, 128),
             held(3 * KX, wide), held(3 * KX, wide), held(3 * CH, wide), held(3 * CH, wide),
             held(3 * CH, slim), held(3 * CH, slim), held(3 * CH, slim), held(3 * CH, slim),
-            held(parts, group, 16, LANES), held(parts, group, 16, LANES),
-            held(parts, ring, 16, LANES), held(parts, ring, 16, LANES),
-            held(parts, group, 16, LANES),
+            held(parts, group, TALL, LANES), held(parts, group, TALL, LANES),
+            held(parts, ring, TALL, LANES), held(parts, ring, TALL, LANES),
+            held(parts, group, TALL, LANES),
             pltpu.SemaphoreType.DMA((5,)), pltpu.SemaphoreType.DMA((parts,)),
             pltpu.SemaphoreType.DMA((11,)), pltpu.SemaphoreType.DMA((11,)),
         ] + [pltpu.SemaphoreType.DMA((parts,))] * 8,
@@ -632,7 +645,7 @@
         in_specs=[anywhere] * 3,
         out_specs=(hbm,) * 4,
         scratch_shapes=[
-            held(parts, group, 16, LANES),
+            held(parts, group, TALL, LANES),
             pltpu.VMEM((9, CH, CIN), F32), pltpu.VMEM((9, CH, CH), F32),
             pltpu.SemaphoreType.DMA, pltpu.SemaphoreType.DMA((4,)),
         ],

time: 41.8 us -> 41.6 us (level)
  no operation moved by 1% of the time
where the time goes in v8:
time: 41.6 us; the launch traced here: 41.4 us
  Pallas kernels  40.8 us (98%)
  between operations  0.64 us (2%)
    pallas_call x1, Pallas kernels, body(): pl.pallas_call(functools.partial(kernel, dims), out_shape=fields_like + (...  39.6 us
    pallas_call x1, Pallas kernels, body(): pl.pallas_call(functools.partial(finish, factor, parts, group), out_shape...  1.17 us

profile of v8, /device:TPU:1, one launch (start us, length us, event | category | flops | bytes accessed | tf_op | source)
XLA Modules:
  0.0 41.4 jit_solution(1604262882650801680)
XLA Ops:
  0.6 39.6 %shard_map.84 = (bf16[48,8,128]{2,1,0:T(8,128)(2,1)S(1)}, bf16[75,8,128]{2,1,0:T(8,128)(2,1)S(1)}, bf16[2,8,32,128]{3,2,1,0:T(8,128)(2,1)S(1)}) custom-call(bf16[75,8,128]{2,1,0:T(8,128)(2,1)} %x_hbm.1, s32[8,128]{1,0:T(8,128)} %m_hbm.1, bf16[9,48,75]{2,1,0:T(8,128)(2,1)} %w1_hbm.1, bf16[9,48,48]{2,1,0:T(8,128)(2,1)} %w2_hbm.1, bf16[48,8,128]{2,1,0:T(8,128)(2,1)} %c_hbm.1), custom_call_target="tpu_custom_call" | custom-call | tf_op jit(solution)/shard_map/pallas_call | solution.py:614
  40.3 1.2 %shard_map.85 = (bf16[48,8,128]{2,1,0:T(8,128)(2,1)}, bf16[75,8,128]{2,1,0:T(8,128)(2,1)}, f32[9,48,75]{2,1,0:T(8,128)}, f32[9,48,48]{2,1,0:T(8,128)}) custom-call(bf16[48,8,128]{2,1,0:T(8,128)(2,1)S(1)} %get-tuple-element.7.out_in, bf16[75,8,128]{2,1,0:T(8,128)(2,1)S(1)} %get-tuple-element.8.dx_in, bf16[2,8,32,128]{3,2,1,0:T(8,128)(2,1)S(1)} %get-tuple-element.9.dw_in), custom_call_target="tpu_custom_call" | custom-call | tf_op jit(solution)/shard_map/pallas_call | solution.py:639

commit v9 on v8

--- a/solution.py
+++ b/solution.py
@@ -445,8 +445,8 @@
     by_z = {j: at_z(j) for j in range(1, z_n)}
     by_y = {j: at_y(j) for j in range(1, y_n)}
     axes = ((z_n, z, by_z.get), (y_n, y, by_y.get))
-    first = [axes[p % 2] for p in range(parts)]
-    second = [axes[1 - p % 2] for p in range(parts)]
+    first = [axes[1 - p % 2] for p in range(parts)]
+    second = [axes[p % 2] for p in range(parts)]
 
     by_x = {j: at_x(j) for j in range(1, group)}
     for p in range(parts):

time: 41.6 us -> 41.6 us (level)
  no operation moved by 1% of the time
where the time goes in v9:
time: 41.6 us; the launch traced here: 41.5 us
  Pallas kernels  40.9 us (98%)
  between operations  0.64 us (2%)
    pallas_call x1, Pallas kernels, body(): pl.pallas_call(functools.partial(kernel, dims), out_shape=fields_like + (...  39.7 us
    pallas_call x1, Pallas kernels, body(): pl.pallas_call(functools.partial(finish, factor, parts, group), out_shape...  1.17 us

profile of v9, /device:TPU:1, one launch (start us, length us, event | category | flops | bytes accessed | tf_op | source)
XLA Modules:
  0.0 41.5 jit_solution(5427615255149322614)
XLA Ops:
  0.6 39.7 %shard_map.84 = (bf16[48,8,128]{2,1,0:T(8,128)(2,1)S(1)}, bf16[75,8,128]{2,1,0:T(8,128)(2,1)S(1)}, bf16[2,8,32,128]{3,2,1,0:T(8,128)(2,1)S(1)}) custom-call(bf16[75,8,128]{2,1,0:T(8,128)(2,1)} %x_hbm.1, s32[8,128]{1,0:T(8,128)} %m_hbm.1, bf16[9,48,75]{2,1,0:T(8,128)(2,1)} %w1_hbm.1, bf16[9,48,48]{2,1,0:T(8,128)(2,1)} %w2_hbm.1, bf16[48,8,128]{2,1,0:T(8,128)(2,1)} %c_hbm.1), custom_call_target="tpu_custom_call" | custom-call | tf_op jit(solution)/shard_map/pallas_call | solution.py:614
  40.3 1.2 %shard_map.85 = (bf16[48,8,128]{2,1,0:T(8,128)(2,1)}, bf16[75,8,128]{2,1,0:T(8,128)(2,1)}, f32[9,48,75]{2,1,0:T(8,128)}, f32[9,48,48]{2,1,0:T(8,128)}) custom-call(bf16[48,8,128]{2,1,0:T(8,128)(2,1)S(1)} %get-tuple-element.7.out_in, bf16[75,8,128]{2,1,0:T(8,128)(2,1)S(1)} %get-tuple-element.8.dx_in, bf16[2,8,32,128]{3,2,1,0:T(8,128)(2,1)S(1)} %get-tuple-element.9.dw_in), custom_call_target="tpu_custom_call" | custom-call | tf_op jit(solution)/shard_map/pallas_call | solution.py:639
